TPU v7x, 768 devices: a whole 4x8x12 slice. The times are simulated.
768 devices in a mesh: wide: 64 (over x, y, core), narrow: 12 (over z).
Axes of the slice: x: 4, y: 8, z: 12, core: 2. Of those that a mesh axis runs over, the one named last changes fastest.
Arguments:
- integrals: bfloat16 [6144, 64, 4096], P(('wide', 'narrow')), may hold values from -0.09375 to 0.09375
- task_shape: int32 [6144], P(('wide', 'narrow')), may hold values from 16 to 64
- task_rows: int32 [6144], P(('wide', 'narrow')), may hold values from 0 to 11
- task_cols: int32 [6144], P(('wide', 'narrow')), may hold values from 0 to 63
- tile_owner: int32 [64], replicated, may hold values from 0 to 63, each once
- amplitudes: bfloat16 [64, 16, 4096], P('wide'), may hold values from -6 to 6
Outputs:
- ladder: float32 [16, 49152], P(None, ('wide', 'narrow'))
Inputs may be any that keep to these rules, and one draw needn't show every extreme that they name: `tile_owner`: each slot once.
All inputs are finite; a program needn't handle non-finite values.
Results may differ from a plain program's by a relative error of at most 0.0003.
Values may be sent and summed in bfloat16 or wider, within the bound.
No kernel may reach another device: no remote copies, remote signals or barrier semaphores. Data moves between devices by JAX's collectives and lax.ppermute only.
A program may use at most 32 MiB of HBM per device.

v0:
```python
import jax
import jax.numpy as jnp
from jax import lax
from jax.sharding import PartitionSpec as P

ROW_DEV = 1


def local(integrals, task_shape, task_rows, task_cols, tile_owner, amplitudes):
    task_count, tile_width, _ = integrals.shape
    pairs_count = amplitudes.shape[1]
    narrow_count = lax.axis_size("narrow")
    slot_ids = jnp.take(tile_owner, task_cols, axis=0)
    gathered = lax.all_gather(amplitudes, "wide", axis=0, tiled=True)
    needed = jnp.take(gathered, slot_ids, axis=0)
    partial_value = jnp.einsum(
        "tbx,tpx->tpb", integrals, needed, preferred_element_type=jnp.float32
    )
    live_rows = lax.broadcasted_iota(jnp.int32, (task_count, tile_width), 1) < task_shape[:, None]
    partial_value = jnp.where(live_rows[:, None, :], partial_value, 0.0)
    row_count = narrow_count * ROW_DEV
    one_hot = (
        task_rows[:, None] == lax.broadcasted_iota(jnp.int32, (task_count, row_count), 1)
    ).astype(jnp.float32)
    buffer = jnp.einsum("tr,tpb->prb", one_hot, partial_value, precision=lax.Precision.HIGHEST)
    buffer = buffer.reshape(pairs_count, row_count * tile_width)
    return lax.psum_scatter(buffer, "narrow", scatter_dimension=1, tiled=True)


def solution(mesh):
    placed = (
        P(("wide", "narrow"), None, None),
        P(("wide", "narrow")),
        P(("wide", "narrow")),
        P(("wide", "narrow")),
        P(),
        P("wide", None, None),
    )
    return jax.shard_map(
        local, mesh=mesh, in_specs=placed, out_specs=P(None, ("wide", "narrow")), check_vma=False
    )
```

profile of v0, /device:TPU:6, one launch (start us, length us, event | category | flops | bytes accessed | tf_op | source)
XLA Modules:
  0.0 183.3 jit_solution(8000893976843604456)
XLA Ops:
  6.5 0.0 copy-start
  6.5 0.0 copy-start.1
  6.5 0.0 all-gather.2.cloned.1.call-start
  6.5 0.7 all-gather.2.cloned.1.call-update
  7.3 0.0 reduce-scatter.4.cloned.1.call-start
  7.3 0.7 compare_select_fusion.1
  8.0 0.0 copy-done
  8.0 0.6 gather_fusion
  8.6 0.7 compare_and_fusion
  9.3 0.7 iota_compare_fusion.1
  10.0 99.8 %all-gather.2.cloned.1.call-done = bf16[64,16,4096]{2,1,0:T(8,128)(2,1)} async-done(((bf16[1,16,4096]{2,1,0:T(8,128)(2,1)}), bf16[64,16,4096]{2,1,0:T(8,128)(2,1)}) %all-gather.2.cloned.1.call-update) | async-done | bytes 8388624 | tf_op jit(solution)/shard_map/all_gather | solution.py:14
  109.8 4.0 %gather_fusion.1 = bf16[8,16,4096]{2,1,0:T(8,128)(2,1)S(1)} fusion(bf16[64,16,4096]{2,1,0:T(8,128)(2,1)} %all-gather.2.cloned.1.call-done, s32[1024]{0:T(1024)S(1)} %pad_clamp_fusion), kind=kCustom, calls=%fused_computation.1 | custom fusion | bytes 2097184 | tf_op jit(solution)/shard_map/jit(_take)/gather | solution.py:15
  113.8 3.5 %convolution_select_fusion = f32[8,16,64]{2,1,0:T(8,128)S(1)} fusion(bf16[8,64,4096]{2,1,0:T(8,128)(2,1)} %param.6, bf16[8,16,4096]{2,1,0:T(8,128)(2,1)S(1)} %gather_fusion.1, pred[8]{0:T(512)(128)(4,1)S(1)} %get-tuple-element.5, pred[8,64]{1,0:T(8,128)(4,1)S(1)} %iota_compare_fusion.1), kind=kOutput, calls=%fused_computation.3 | convolution fusion | flops 67641344 | bytes 5276168 | tf_op jit(solution)/shard_map/tbx,tpx->tpb/dot_general | solution.py:16
  117.2 0.0 copy-done.1
  117.2 0.3 convolution_bitcast_fusion
  117.6 0.9 copy.10
  118.5 0.0 reduce-scatter.4.cloned.1.call-update
  118.6 56.5 %reduce-scatter.4.cloned.1.call-done = f32[64,16]{1,0:T(8,128)} async-done(((f32[768,16]{1,0:T(8,128)}), f32[64,16]{1,0:T(8,128)}) %reduce-scatter.4.cloned.1.call-update) | async-done | bytes 4112
  175.0 1.4 copy.9
  (2 shorter events, 0.0 us)
Async XLA Ops:
  6.5 1.4 copy-start
  6.5 110.7 %copy-start.1 = (s32[8]{0:T(128)S(1)}, s32[8]{0:T(128)}, u32[]{:S(2)}) copy-start(s32[8]{0:T(128)} %param.8) | copy-start | bytes 100
  6.5 103.3 %all-gather.2.cloned.1.call-start = ((), (), s32[]{:S(2)}) async-start(), calls=%async_computation.1 | async-start | bytes 8519680 | tf_op jit(solution)/shard_map/all_gather | solution.py:14
  7.3 167.7 %reduce-scatter.4.cloned.1.call-start = ((), (), s32[]{:S(2)}) async-start(), calls=%async_computation.2 | async-start | bytes 425984
Sparse Core Ops, SparseCore 0:
  11.3 98.4 all-gather.1
  118.7 56.2 reduce-scatter.3
where the time goes:
time: 184 us; the launch traced here: 183 us
  waiting for transfers between devices  157 us (85%)
  between operations  13.4 us (7%)
  local copies, waits for them, and re-layouts  7.01 us (4%)
  matrix products  3.79 us (2%)
  other arithmetic  2.07 us (1%)
    all_gather x1, waiting for transfers between devices, local(): gathered = lax.all_gather(amplitudes, 'wide', axis=0, tiled=True)  99.8 us
    unnamed x3, waiting for transfers between devices  57.2 us
    gather x1, local copies, waits for them, and re-layouts, local(): needed = jnp.take(gathered, slot_ids, axis=0)  3.99 us
  transfers between devices with their start and end apart: 2, of which 2 were waited for; matrix products, arithmetic and copies ran while one was open for 1% of the time, Pallas kernels for 0%

commit v1 on v0

v1 whole, which is shorter than its diff:
```python
import jax
import jax.numpy as jnp
from jax import lax
from jax.sharding import PartitionSpec as P

XS, YH, YL, CORES = 4, 4, 2, 2
GROUP = XS * YL * CORES
LANES = 128


def local(integrals, task_shape, task_rows, task_cols, tile_owner, amplitudes):
    tasks, tile_width, depth = integrals.shape
    pairs = amplitudes.shape[1]
    narrow = lax.axis_size("narrow")
    wide = lax.axis_size("wide")
    part = depth // GROUP
    halves = part // LANES
    payload = halves * pairs
    groups = [
        [((x * YH + yh) * YL + yl) * CORES + c for x in range(XS) for yl in range(YL) for c in range(CORES)]
        for yh in range(YH)
    ]

    slots = jnp.take(tile_owner, task_cols, axis=0)
    slices = amplitudes.reshape(pairs, GROUP, halves, LANES).transpose(1, 2, 0, 3)
    slices = slices.reshape(GROUP, payload, LANES)
    wanted = jnp.broadcast_to(slots.astype(amplitudes.dtype)[None, :, None], (GROUP, tasks, LANES))
    blocks = jnp.concatenate([slices, wanted], axis=1)
    blocks = blocks.reshape(XS, 1, YL, CORES, payload + tasks, LANES)
    blocks = jnp.broadcast_to(blocks, (XS, YH, YL, CORES, payload + tasks, LANES))
    blocks = blocks.reshape(wide, payload + tasks, LANES)
    have = lax.all_to_all(blocks, "wide", 0, 0, tiled=True)

    yh = (lax.axis_index("wide") // (YL * CORES)) % YH
    asked = have[:, payload:, 0].reshape(XS, YH, YL * CORES, tasks)
    asked = lax.dynamic_index_in_dim(asked, yh, 1, keepdims=False).reshape(GROUP * tasks)
    chosen = jnp.take(have[:, :payload], asked.astype(jnp.int32), axis=0)
    chosen = chosen.reshape(GROUP, tasks * payload, LANES)
    needed = lax.all_to_all(chosen, "wide", 0, 0, axis_index_groups=groups, tiled=True)
    needed = needed.reshape(GROUP, tasks, halves, pairs, LANES).transpose(1, 3, 0, 2, 4)
    needed = needed.reshape(tasks, pairs, depth)

    partial = jnp.einsum("tbx,tpx->tpb", integrals, needed, preferred_element_type=jnp.float32)
    live = lax.broadcasted_iota(jnp.int32, (tasks, tile_width), 1) < task_shape[:, None]
    partial = jnp.where(live[:, None, :], partial, 0.0)
    one_hot = (task_rows[:, None] == lax.broadcasted_iota(jnp.int32, (tasks, narrow), 1)).astype(jnp.float32)
    rows = jnp.einsum("tr,tpb->rpb", one_hot, partial, precision=lax.Precision.HIGHEST)
    rows = lax.all_to_all(rows, "narrow", 0, 0, tiled=True)
    return jnp.sum(rows, axis=0)


def solution(mesh):
    placed = (
        P(("wide", "narrow"), None, None),
        P(("wide", "narrow")),
        P(("wide", "narrow")),
        P(("wide", "narrow")),
        P(),
        P("wide", None, None),
    )
    return jax.shard_map(
        local, mesh=mesh, in_specs=placed, out_specs=P(None, ("wide", "narrow")), check_vma=False
    )
```

time: 184 us -> 91.9 us (0.50)
  the two profiles are of different devices: /device:TPU:6 before, /device:TPU:1 now
where the time goes in v1:
time: 91.9 us; the launch traced here: 91.5 us
  waiting for transfers between devices  35.9 us (39%)
  blocking collectives  21.3 us (23%)
  starting transfers between devices  19.5 us (21%)
  local copies, waits for them, and re-layouts  6.43 us (7%)
  other arithmetic  4.44 us (5%)
  matrix products  3.77 us (4%)
    all_to_all x1, blocking collectives, local(): rows = lax.all_to_all(rows, 'narrow', 0, 0, tiled=True)  21.3 us
    all_to_all x1, waiting for transfers between devices, local(): have = lax.all_to_all(blocks, 'wide', 0, 0, tiled=True)  20.1 us
    all_to_all x1, waiting for transfers between devices, local(): lax.all_to_all(chosen, 'wide', 0, 0, axis_index_groups=groups, tiled=True)  15.7 us
    all_to_all x1, starting transfers between devices, local(): have = lax.all_to_all(blocks, 'wide', 0, 0, tiled=True)  14.7 us
    all_to_all x1, starting transfers between devices, local(): lax.all_to_all(chosen, 'wide', 0, 0, axis_index_groups=groups, tiled=True)  4.83 us
    dot_general x1, matrix products, local(): jnp.einsum('tbx,tpx->tpb', integrals, needed, preferred_element_type=jnp....  3.44 us
  transfers between devices with their start and end apart: 2, of which 2 were waited for; matrix products, arithmetic and copies ran while one was open for 0% of the time, Pallas kernels for 0%

profile of v1, /device:TPU:1, one launch (start us, length us, event | category | flops | bytes accessed | tf_op | source)
XLA Modules:
  0.0 91.5 jit_solution(10630606195273177013)
XLA Ops:
  0.0 0.0 copy-start
  0.0 1.0 %reshape.80 = bf16[16,16,2,128]{3,2,1,0:T(2,128)(2,1)S(1)} reshape(bf16[1,16,4096]{2,1,0:T(8,128)(2,1)} %param.11) | data formatting | bytes 262144 | tf_op jit(solution)/shard_map/reshape | solution.py:25
  1.0 0.1 copy.11
  1.1 0.7 compare_select_fusion.2
  1.7 0.0 copy-done
  1.7 0.6 gather_fusion
  2.4 0.7 fusion.6
  3.0 0.1 pad.1.clone
  3.1 0.1 maximum_bitcast_fusion
  3.2 0.9 %broadcast_in_dim.50 = bf16[4,4,2,2,40,128]{5,4,3,2,1,0:T(8,128)(2,1)} broadcast(bf16[4,2,2,40,128]{4,3,2,1,0:T(8,128)(2,1)S(1)} %maximum_bitcast_fusion), dimensions={0,2,3,4,5} | broadcast | bytes 819200 | tf_op jit(solution)/shard_map/broadcast_in_dim | solution.py:30
  4.1 0.0 copy-start.2
  4.1 14.7 %all-to-all-start = ((bf16[64,40,128]{2,1,0:T(8,128)(2,1)}), bf16[64,40,128]{2,1,0:T(8,128)(2,1)S(1)}, u32[]{:S(2)}, u32[]{:S(2)}) async-start(bf16[64,40,128]{2,1,0:T(8,128)(2,1)} %bitcast.4), calls=%async_computation | async-start | bytes 1310720 | tf_op jit(solution)/shard_map/all_to_all | solution.py:32
  18.9 20.1 %all-to-all-done = bf16[64,40,128]{2,1,0:T(8,128)(2,1)S(1)} async-done(((bf16[64,40,128]{2,1,0:T(8,128)(2,1)}), bf16[64,40,128]{2,1,0:T(8,128)(2,1)S(1)}, u32[]{:S(2)}, u32[]{:S(2)}) %all-to-all-start) | async-done | bytes 655392 | tf_op jit(solution)/shard_map/all_to_all | solution.py:32
  39.0 0.2 slice_reduce_fusion
  39.2 0.1 reshape.85
  39.3 0.1 broadcast_in_dim.51
  39.4 0.1 broadcast_in_dim.52
  39.6 0.8 gather_fusion.1
  40.3 1.5 %bitcast_select_fusion = bf16[16,256,128]{2,1,0:T(8,128)(2,1)} fusion(pred[16,256]{1,0:T(8,128)(4,1)S(1)} %broadcast_in_dim.52, bf16[16,256,128]{2,1,0:T(8,128)(2,1)S(1)} %bitcast.20), kind=kLoop, calls=%fused_computation.3 | loop fusion | flops 524288 | bytes 2101248 | tf_op jit(solution)/shard_map/jit(_take)/select_n | solution.py:37
  41.9 4.8 %all-to-all-start.1 = ((bf16[16,256,128]{2,1,0:T(8,128)(2,1)}), bf16[16,256,128]{2,1,0:T(8,128)(2,1)S(1)}, u32[]{:S(2)}, u32[]{:S(2)}) async-start(bf16[16,256,128]{2,1,0:T(8,128)(2,1)} %bitcast_select_fusion), calls=%async_computation.1 | async-start | bytes 2097152 | tf_op jit(solution)/shard_map/all_to_all | solution.py:39
  46.7 0.0 copy-done.2
  46.7 0.1 iota_compare_fusion
  46.8 15.7 %all-to-all-done.1 = bf16[16,256,128]{2,1,0:T(8,128)(2,1)S(1)} async-done(((bf16[16,256,128]{2,1,0:T(8,128)(2,1)}), bf16[16,256,128]{2,1,0:T(8,128)(2,1)S(1)}, u32[]{:S(2)}, u32[]{:S(2)}) %all-to-all-start.1) | async-done | bytes 1048608 | tf_op jit(solution)/shard_map/all_to_all | solution.py:39
  62.5 0.9 %copy.12 = bf16[8,16,16,2,128]{4,3,2,1,0:T(2,128)(2,1)S(1)} copy(bf16[8,16,16,2,128]{4,1,3,0,2:T(8,128)(2,1)S(1)} %bitcast.21) | data formatting | bytes 2097152 | tf_op jit(solution)/shard_map/transpose | solution.py:40
  63.5 0.0 copy-start.1
  63.5 0.8 reshape.83
  64.3 3.4 %convolution_select_fusion = f32[8,16,64]{2,1,0:T(8,128)S(1)} fusion(bf16[8,16,4096]{2,1,0:T(8,128)(2,1)S(1)} %reshape.83, bf16[8,64,4096]{2,1,0:T(8,128)(2,1)} %param.6, pred[8,64]{1,0:T(8,128)(4,1)S(1)} %iota_compare_fusion), kind=kOutput, calls=%fused_computation.2 | convolution fusion | flops 67117056 | bytes 5276160 | tf_op jit(solution)/shard_map/tbx,tpx->tpb/dot_general | solution.py:43
  67.8 0.0 copy-done.1
  67.8 0.3 fusion
  68.1 0.1 reshape.106
  68.3 21.3 %all_to_all.15 = f32[12,1,1024]{2,1,0:T(1,128)S(1)} all-to-all(f32[12,1,1024]{2,1,0:T(1,128)S(1)} %reshape.106), channel_id=1, replica_groups=mesh['wide'=64,'narrow'=12] {'narrow'}, dimensions={0} | all-to-all | bytes 98304 | tf_op jit(solution)/shard_map/all_to_all | solution.py:48
  89.5 0.5 broadcast.69
  90.1 0.8 reduce.2
  90.8 0.1 reshape.107
  90.9 0.6 reduce_sum.9
  (7 shorter events, 0.1 us)
Async XLA Ops:
  0.0 1.7 %copy-start = (s32[64]{0:T(128)S(1)}, s32[64]{0:T(128)}, u32[]{:S(2)}) copy-start(s32[64]{0:T(128)} %param.10) | copy-start | bytes 772
  4.1 42.6 %copy-start.2 = (s32[8]{0:T(128)S(1)}, s32[8]{0:T(128)}, u32[]{:S(2)}) copy-start(s32[8]{0:T(128)} %param.7) | copy-start | bytes 100
  4.1 34.9 %all-to-all-start = ((bf16[64,40,128]{2,1,0:T(8,128)(2,1)}), bf16[64,40,128]{2,1,0:T(8,128)(2,1)S(1)}, u32[]{:S(2)}, u32[]{:S(2)}) async-start(bf16[64,40,128]{2,1,0:T(8,128)(2,1)} %bitcast.4), calls=%async_computation | async-start | bytes 1310720 | tf_op jit(solution)/shard_map/all_to_all | solution.py:32
  41.9 20.7 %all-to-all-start.1 = ((bf16[16,256,128]{2,1,0:T(8,128)(2,1)}), bf16[16,256,128]{2,1,0:T(8,128)(2,1)S(1)}, u32[]{:S(2)}, u32[]{:S(2)}) async-start(bf16[16,256,128]{2,1,0:T(8,128)(2,1)} %bitcast_select_fusion), calls=%async_computation.1 | async-start | bytes 2097152 | tf_op jit(solution)/shard_map/all_to_all | solution.py:39
  63.5 4.3 %copy-start.1 = (s32[8]{0:T(128)S(1)}, s32[8]{0:T(128)}, u32[]{:S(2)}) copy-start(s32[8]{0:T(128)} %param.8) | copy-start | bytes 100

commit v2 on v1

v2 whole, which is shorter than its diff:
```python
import jax
import jax.numpy as jnp
from jax import lax
from jax.experimental import pallas as pl
from jax.experimental.pallas import tpu as pltpu
from jax.sharding import PartitionSpec as P

XS, YH, YL, CORES = 4, 4, 2, 2
NEAR = YL * CORES
GROUP = XS * NEAR
LANES = 128
VMEM = pl.BlockSpec(memory_space=pltpu.VMEM)
SMEM = pl.BlockSpec(memory_space=pltpu.SMEM)


def spread_kernel(cols_ref, owner_ref, amp_ref, out_ref):
    tasks = cols_ref.shape[0]
    _, pairs, depth = amp_ref.shape
    part = depth // GROUP
    payload = part // LANES * pairs
    rows = out_ref.shape[1] - payload
    lane = lax.broadcasted_iota(jnp.int32, (rows, LANES), 1)
    wanted = jnp.zeros((rows, LANES), jnp.float32)
    for s in range(tasks):
        wanted = jnp.where(lane == s, owner_ref[cols_ref[s]].astype(jnp.float32), wanted)
    wanted = wanted.astype(out_ref.dtype)
    for j in range(GROUP):
        x, near = divmod(j, NEAR)
        for yh in range(YH):
            w = (x * YH + yh) * NEAR + near
            for h in range(part // LANES):
                at = j * part + h * LANES
                out_ref[w, h * pairs : (h + 1) * pairs, :] = amp_ref[0, :, at : at + LANES]
            out_ref[w, payload:, :] = wanted


def select_kernel(asked_ref, have_ref, out_ref):
    payload = out_ref.shape[1]

    def copy(i, carry):
        out_ref[i] = have_ref[asked_ref[i], :payload, :]
        return carry

    lax.fori_loop(0, out_ref.shape[0], copy, 0, unroll=8)


def ladder_kernel(shape_ref, rows_ref, integrals_ref, needed_ref, out_ref, weight_ref):
    step, steps = pl.program_id(0), pl.num_programs(0)
    some, width, depth = integrals_ref.shape
    tasks = shape_ref.shape[0]
    members, per, _ = needed_ref.shape
    halves = depth // members // LANES
    pairs = per // tasks // halves

    @pl.when(step == 0)
    def _():
        out_ref[...] = jnp.zeros_like(out_ref)
        for s in range(tasks):
            for j in range(members):
                for h in range(halves):
                    at = (j * halves + h) * LANES
                    row = (s * halves + h) * pairs
                    weight_ref[s, :, at : at + LANES] = needed_ref[j, row : row + pairs, :]

    for i in range(some):
        t = step * some + i
        product = lax.dot_general(
            weight_ref[t], integrals_ref[i], (((1,), (1,)), ((), ())), preferred_element_type=jnp.float32
        )
        live = lax.broadcasted_iota(jnp.int32, product.shape, 1) < shape_ref[t]
        product = jnp.where(live, product, 0.0)
        packed = jnp.concatenate([product[: pairs // 2], product[pairs // 2 :]], axis=1)
        out_ref[rows_ref[t]] += packed


def local(integrals, task_shape, task_rows, task_cols, tile_owner, amplitudes):
    tasks, width, depth = integrals.shape
    pairs = amplitudes.shape[1]
    narrow = lax.axis_size("narrow")
    wide = lax.axis_size("wide")
    payload = depth // GROUP // LANES * pairs
    kind = amplitudes.dtype
    groups = [[(x * YH + yh) * NEAR + near for x in range(XS) for near in range(NEAR)] for yh in range(YH)]

    blocks = pl.pallas_call(
        spread_kernel,
        out_shape=jax.ShapeDtypeStruct((wide, payload + 8, LANES), kind),
        in_specs=[SMEM, SMEM, VMEM],
        out_specs=VMEM,
    )(task_cols, tile_owner, amplitudes)
    have = lax.all_to_all(blocks, "wide", 0, 0, tiled=True)

    yh = lax.div(lax.axis_index("wide"), NEAR) % YH
    asked = have[:, payload, :tasks].reshape(XS, YH, NEAR, tasks)
    asked = lax.dynamic_index_in_dim(asked, yh, 1, keepdims=False).reshape(GROUP * tasks)
    chosen = pl.pallas_call(
        select_kernel,
        out_shape=jax.ShapeDtypeStruct((GROUP * tasks, payload, LANES), kind),
        in_specs=[SMEM, VMEM],
        out_specs=VMEM,
    )(asked.astype(jnp.int32), have)
    chosen = chosen.reshape(GROUP, tasks * payload, LANES)
    needed = lax.all_to_all(chosen, "wide", 0, 0, axis_index_groups=groups, tiled=True)

    some = 2
    rows = pl.pallas_call(
        ladder_kernel,
        out_shape=jax.ShapeDtypeStruct((narrow, pairs // 2, 2 * width), jnp.float32),
        grid_spec=pltpu.PrefetchScalarGridSpec(
            num_scalar_prefetch=2,
            grid=(tasks // some,),
            in_specs=[
                pl.BlockSpec((some, width, depth), lambda i, *_: (i, 0, 0)),
                pl.BlockSpec(needed.shape, lambda i, *_: (0, 0, 0)),
            ],
            out_specs=pl.BlockSpec((narrow, pairs // 2, 2 * width), lambda i, *_: (0, 0, 0)),
            scratch_shapes=[pltpu.VMEM((tasks, pairs, depth), kind)],
        ),
        compiler_params=pltpu.CompilerParams(vmem_limit_bytes=32 * 1024 * 1024),
    )(task_shape, task_rows, integrals, needed)
    rows = lax.all_to_all(rows, "narrow", 0, 0, tiled=True)
    total = jnp.sum(rows, axis=0)
    return jnp.concatenate([total[:, :width], total[:, width:]], axis=0)


def solution(mesh):
    placed = (
        P(("wide", "narrow"), None, None),
        P(("wide", "narrow")),
        P(("wide", "narrow")),
        P(("wide", "narrow")),
        P(),
        P("wide", None, None),
    )
    return jax.shard_map(
        local, mesh=mesh, in_specs=placed, out_specs=P(None, ("wide", "narrow")), check_vma=False
    )
```

time: 91.9 us -> 87.4 us (0.951)
  blocking collectives: 21.3 us -> 41.5 us
  waiting for transfers between devices: 35.9 us -> 20.1 us
  Pallas kernels: 0 us -> 6.7 us
  starting transfers between devices: 19.5 us -> 14.6 us
  other arithmetic: 4.44 us -> 0.63 us
  matrix products: 3.77 us -> 0 us
  local copies, waits for them, and re-layouts: 6.43 us -> 3.1 us
    all_to_all x0 -> x1, blocking collectives: none -> 20.2 us  [local(): lax.all_to_all(chosen, 'wide', 0, 0, axis_index_groups=groups, tiled=True)]
    all_to_all x1 -> x0, waiting for transfers between devices: 15.7 us -> none  [local(): lax.all_to_all(chosen, 'wide', 0, 0, axis_index_groups=groups, tiled=True)]
    pallas_call x0 -> x3, Pallas kernels: none -> 6.7 us  [the longest x1 2.55 us: local(): pl.pallas_call(ladder_kernel, out_shape=jax.ShapeDtypeStruct((narrow, pai...]
    all_to_all x1 -> x0, starting transfers between devices: 4.83 us -> none  [local(): lax.all_to_all(chosen, 'wide', 0, 0, axis_index_groups=groups, tiled=True)]
    dot_general x2 -> x0, matrix products: 3.77 us -> none  [the longest x1 3.44 us: local(): jnp.einsum('tbx,tpx->tpb', integrals, needed, preferred_element_type=jnp....]
    select_n x3 -> x0, other arithmetic: 2.19 us -> none  [the longest x2 1.53 us: local(): chosen = jnp.take(have[:, :payload], asked.astype(jnp.int32), axis=0)]
    unnamed x8 -> x9, local copies, waits for them, and re-layouts: 0.21 us -> 2.34 us
    reshape x2 -> x0, local copies, waits for them, and re-layouts: 1.81 us -> none  [the longest x1 0.99 us: local(): amplitudes.reshape(pairs, GROUP, halves, LANES).transpose(1, 2, 0, 3)]
  transfers between devices with their start and end apart: 2 -> 1, of which waited for: 2 -> 1; matrix products, arithmetic and copies ran while one was open for 0% -> 0% of each run, Pallas kernels for 0% -> 0%
where the time goes in v2:
time: 87.4 us; the launch traced here: 86.7 us
  blocking collectives  41.5 us (47%)
  waiting for transfers between devices  20.1 us (23%)
  starting transfers between devices  14.6 us (17%)
  Pallas kernels  6.7 us (8%)
  local copies, waits for them, and re-layouts  3.1 us (4%)
    all_to_all x1, blocking collectives, local(): rows = lax.all_to_all(rows, 'narrow', 0, 0, tiled=True)  21.3 us
    all_to_all x1, blocking collectives, local(): lax.all_to_all(chosen, 'wide', 0, 0, axis_index_groups=groups, tiled=True)  20.2 us
    all_to_all x1, waiting for transfers between devices, local(): have = lax.all_to_all(blocks, 'wide', 0, 0, tiled=True)  20.1 us
    all_to_all x1, starting transfers between devices, local(): have = lax.all_to_all(blocks, 'wide', 0, 0, tiled=True)  14.6 us
    pallas_call x1, Pallas kernels, local(): pl.pallas_call(ladder_kernel, out_shape=jax.ShapeDtypeStruct((narrow, pai...  2.55 us
    unnamed x9, local copies, waits for them, and re-layouts  2.34 us
    pallas_call x1, Pallas kernels, local(): pl.pallas_call(select_kernel, out_shape=jax.ShapeDtypeStruct((GROUP * tas...  2.28 us
    pallas_call x1, Pallas kernels, local(): pl.pallas_call(spread_kernel, out_shape=jax.ShapeDtypeStruct((wide, paylo...  1.87 us
  transfers between devices with their start and end apart: 1, of which 1 were waited for; matrix products, arithmetic and copies ran while one was open for 0% of the time, Pallas kernels for 0%

profile of v2, /device:TPU:1, one launch (start us, length us, event | category | flops | bytes accessed | tf_op | source)
XLA Modules:
  0.0 86.7 jit_solution(8480124895157852625)
XLA Ops:
  0.0 0.0 copy-start.2
  0.0 0.0 copy-start.1
  0.0 1.9 %shard_map.64 = bf16[64,40,128]{2,1,0:T(8,128)(2,1)} custom-call(s32[8]{0:T(128)} %cols_ref.1, s32[64]{0:T(128)} %owner_ref.1, bf16[1,16,4096]{2,1,0:T(8,128)(2,1)} %amp_ref.1), custom_call_target="tpu_custom_call" | custom-call | tf_op jit(solution)/shard_map/pallas_call | solution.py:85
  1.9 14.6 %all-to-all-start = ((bf16[64,40,128]{2,1,0:T(8,128)(2,1)}), bf16[64,40,128]{2,1,0:T(8,128)(2,1)S(1)}, u32[]{:S(2)}, u32[]{:S(2)}) async-start(bf16[64,40,128]{2,1,0:T(8,128)(2,1)} %shard_map.64), calls=%async_computation | async-start | bytes 1310720 | tf_op jit(solution)/shard_map/all_to_all | solution.py:91
  16.5 20.1 %all-to-all-done.have_ref = bf16[64,40,128]{2,1,0:T(8,128)(2,1)S(1)} async-done(((bf16[64,40,128]{2,1,0:T(8,128)(2,1)}), bf16[64,40,128]{2,1,0:T(8,128)(2,1)S(1)}, u32[]{:S(2)}, u32[]{:S(2)}) %all-to-all-start) | async-done | bytes 655392 | tf_op jit(solution)/shard_map/all_to_all | solution.py:91
  36.6 0.0 copy-start.3
  36.7 0.7 reshape.8.asked_ref
  37.4 0.1 copy-done.3
  37.5 2.3 %shard_map.65 = bf16[128,32,128]{2,1,0:T(8,128)(2,1)} custom-call(s32[128]{0:T(128)} %reshape.8.asked_ref, bf16[64,40,128]{2,1,0:T(8,128)(2,1)} %copy-done.3), custom_call_target="tpu_custom_call" | custom-call | tf_op jit(solution)/shard_map/pallas_call | solution.py:96
  39.8 20.2 %all_to_all.15.needed_ref = bf16[16,256,128]{2,1,0:T(8,128)(2,1)S(1)} all-to-all(bf16[16,256,128]{2,1,0:T(8,128)(2,1)} %bitcast.2), channel_id=1, replica_groups={{0,12,24,36,192,204,216,228,384,396,408,420,576,588,600,612},{48,60,72,..., dimensions={0} | all-to-all | bytes 2097152 | tf_op jit(solution)/shard_map/all_to_all | solution.py:103
  60.0 0.0 copy-done.2
  60.0 0.0 copy-done.1
  60.0 0.0 copy-start
  60.0 2.2 %copy-done = bf16[8,64,4096]{2,1,0:T(8,128)(2,1)S(1)} copy-done((bf16[8,64,4096]{2,1,0:T(8,128)(2,1)S(1)}, bf16[8,64,4096]{2,1,0:T(8,128)(2,1)}, u32[]{:S(2)}) %copy-start) | copy-done | bytes 4194328
  62.2 2.6 %shard_map.66 = f32[12,8,128]{2,1,0:T(8,128)S(1)} custom-call(s32[8]{0:T(128)S(1)} %copy-done.1, s32[8]{0:T(128)S(1)} %copy-done.2, bf16[8,64,4096]{2,1,0:T(8,128)(2,1)S(1)} %copy-done, bf16[16,256,128]{2,1,0:T(8,128)(2,1)S(1)} %all_to_all.15.needed_ref), custom_call_target="tpu_custom_call" | custom-call | tf_op jit(solution)/shard_map/pallas_call | solution.py:106
  64.8 21.3 %all_to_all.16 = f32[12,8,128]{2,1,0:T(8,128)S(1)} all-to-all(f32[12,8,128]{2,1,0:T(8,128)S(1)} %shard_map.66), channel_id=1, replica_groups=mesh['wide'=64,'narrow'=12] {'narrow'}, dimensions={0} | all-to-all | bytes 98304 | tf_op jit(solution)/shard_map/all_to_all | solution.py:121
  86.1 0.1 fusion
  86.1 0.6 pad_maximum_fusion
  (4 shorter events, 0.1 us)
Async XLA Ops:
  0.0 60.0 %copy-start.2 = (s32[8]{0:T(128)S(1)}, s32[8]{0:T(128)}, u32[]{:S(2)}) copy-start(s32[8]{0:T(128)} %rows_ref.1) | copy-start | bytes 100
  0.0 60.0 %copy-start.1 = (s32[8]{0:T(128)S(1)}, s32[8]{0:T(128)}, u32[]{:S(2)}) copy-start(s32[8]{0:T(128)} %shape_ref.1) | copy-start | bytes 100
  1.9 34.8 %all-to-all-start = ((bf16[64,40,128]{2,1,0:T(8,128)(2,1)}), bf16[64,40,128]{2,1,0:T(8,128)(2,1)S(1)}, u32[]{:S(2)}, u32[]{:S(2)}) async-start(bf16[64,40,128]{2,1,0:T(8,128)(2,1)} %shard_map.64), calls=%async_computation | async-start | bytes 1310720 | tf_op jit(solution)/shard_map/all_to_all | solution.py:91
  36.6 0.9 copy-start.3
  60.0 2.2 %copy-start = (bf16[8,64,4096]{2,1,0:T(8,128)(2,1)S(1)}, bf16[8,64,4096]{2,1,0:T(8,128)(2,1)}, u32[]{:S(2)}) copy-start(bf16[8,64,4096]{2,1,0:T(8,128)(2,1)} %integrals_ref.1) | copy-start | bytes 12582916

commit v3 on v2

--- a/solution.py
+++ b/solution.py
@@ -11,6 +11,10 @@
 LANES = 128
 VMEM = pl.BlockSpec(memory_space=pltpu.VMEM)
 SMEM = pl.BlockSpec(memory_space=pltpu.SMEM)
+
+
+def room(mib):
+    return pltpu.CompilerParams(vmem_limit_bytes=mib * 1024 * 1024)
 
 
 def spread_kernel(cols_ref, owner_ref, amp_ref, out_ref):
@@ -44,33 +48,27 @@
     lax.fori_loop(0, out_ref.shape[0], copy, 0, unroll=8)
 
 
-def ladder_kernel(shape_ref, rows_ref, integrals_ref, needed_ref, out_ref, weight_ref):
-    step, steps = pl.program_id(0), pl.num_programs(0)
-    some, width, depth = integrals_ref.shape
-    tasks = shape_ref.shape[0]
+def ladder_kernel(shape_ref, rows_ref, integrals_ref, needed_ref, out_ref):
+    tasks, width, depth = integrals_ref.shape
     members, per, _ = needed_ref.shape
     halves = depth // members // LANES
     pairs = per // tasks // halves
-
-    @pl.when(step == 0)
-    def _():
-        out_ref[...] = jnp.zeros_like(out_ref)
-        for s in range(tasks):
-            for j in range(members):
-                for h in range(halves):
-                    at = (j * halves + h) * LANES
-                    row = (s * halves + h) * pairs
-                    weight_ref[s, :, at : at + LANES] = needed_ref[j, row : row + pairs, :]
-
-    for i in range(some):
-        t = step * some + i
+    out_ref[...] = jnp.zeros_like(out_ref)
+    for t in range(tasks):
+        chosen = [
+            needed_ref[j, (t * halves + h) * pairs : (t * halves + h + 1) * pairs, :]
+            for j in range(members)
+            for h in range(halves)
+        ]
         product = lax.dot_general(
-            weight_ref[t], integrals_ref[i], (((1,), (1,)), ((), ())), preferred_element_type=jnp.float32
+            jnp.concatenate(chosen, axis=1),
+            integrals_ref[t],
+            (((1,), (1,)), ((), ())),
+            preferred_element_type=jnp.float32,
         )
         live = lax.broadcasted_iota(jnp.int32, product.shape, 1) < shape_ref[t]
         product = jnp.where(live, product, 0.0)
-        packed = jnp.concatenate([product[: pairs // 2], product[pairs // 2 :]], axis=1)
-        out_ref[rows_ref[t]] += packed
+        out_ref[rows_ref[t]] += jnp.concatenate([product[: pairs // 2], product[pairs // 2 :]], axis=1)
 
 
 def local(integrals, task_shape, task_rows, task_cols, tile_owner, amplitudes):
@@ -87,6 +85,7 @@
         out_shape=jax.ShapeDtypeStruct((wide, payload + 8, LANES), kind),
         in_specs=[SMEM, SMEM, VMEM],
         out_specs=VMEM,
+        compiler_params=room(2),
     )(task_cols, tile_owner, amplitudes)
     have = lax.all_to_all(blocks, "wide", 0, 0, tiled=True)
 
@@ -98,25 +97,17 @@
         out_shape=jax.ShapeDtypeStruct((GROUP * tasks, payload, LANES), kind),
         in_specs=[SMEM, VMEM],
         out_specs=VMEM,
+        compiler_params=room(3),
     )(asked.astype(jnp.int32), have)
     chosen = chosen.reshape(GROUP, tasks * payload, LANES)
     needed = lax.all_to_all(chosen, "wide", 0, 0, axis_index_groups=groups, tiled=True)
 
-    some = 2
     rows = pl.pallas_call(
         ladder_kernel,
         out_shape=jax.ShapeDtypeStruct((narrow, pairs // 2, 2 * width), jnp.float32),
-        grid_spec=pltpu.PrefetchScalarGridSpec(
-            num_scalar_prefetch=2,
-            grid=(tasks // some,),
-            in_specs=[
-                pl.BlockSpec((some, width, depth), lambda i, *_: (i, 0, 0)),
-                pl.BlockSpec(needed.shape, lambda i, *_: (0, 0, 0)),
-            ],
-            out_specs=pl.BlockSpec((narrow, pairs // 2, 2 * width), lambda i, *_: (0, 0, 0)),
-            scratch_shapes=[pltpu.VMEM((tasks, pairs, depth), kind)],
-        ),
-        compiler_params=pltpu.CompilerParams(vmem_limit_bytes=32 * 1024 * 1024),
+        in_specs=[SMEM, SMEM, VMEM, VMEM],
+        out_specs=VMEM,
+        compiler_params=room(6),
     )(task_shape, task_rows, integrals, needed)
     rows = lax.all_to_all(rows, "narrow", 0, 0, tiled=True)
     total = jnp.sum(rows, axis=0)

time: 87.4 us -> 86 us (0.984)
  Pallas kernels: 6.7 us -> 4.02 us
  local copies, waits for them, and re-layouts: 3.1 us -> 4.6 us
    unnamed x9 -> x13, local copies, waits for them, and re-layouts: 2.34 us -> 4.41 us
    pallas_call x1, Pallas kernels: 2.28 us -> 0.75 us  [local(): pl.pallas_call(select_kernel, out_shape=jax.ShapeDtypeStruct((GROUP * tas...]
where the time goes in v3:
time: 86 us; the launch traced here: 85.4 us
  blocking collectives  41.3 us (48%)
  waiting for transfers between devices  20.1 us (23%)
  starting transfers between devices  14.6 us (17%)
  local copies, waits for them, and re-layouts  4.6 us (5%)
  Pallas kernels  4.02 us (5%)
    all_to_all x1, blocking collectives, local(): rows = lax.all_to_all(rows, 'narrow', 0, 0, tiled=True)  21.3 us
    all_to_all x1, waiting for transfers between devices, local(): have = lax.all_to_all(blocks, 'wide', 0, 0, tiled=True)  20.1 us
    all_to_all x1, blocking collectives, local(): lax.all_to_all(chosen, 'wide', 0, 0, axis_index_groups=groups, tiled=True)  20 us
    all_to_all x1, starting transfers between devices, local(): have = lax.all_to_all(blocks, 'wide', 0, 0, tiled=True)  14.6 us
    unnamed x13, local copies, waits for them, and re-layouts  4.41 us
    pallas_call x1, Pallas kernels, local(): pl.pallas_call(ladder_kernel, out_shape=jax.ShapeDtypeStruct((narrow, pai...  1.8 us
  transfers between devices with their start and end apart: 1, of which 1 were waited for; matrix products, arithmetic and copies ran while one was open for 0% of the time, Pallas kernels for 0%

profile of v3, /device:TPU:1, one launch (start us, length us, event | category | flops | bytes accessed | tf_op | source)
XLA Modules:
  0.0 85.4 jit_solution(14353113773532013334)
XLA Ops:
  0.0 0.0 copy-start.1
  0.0 0.9 %copy-done.1 = bf16[1,16,4096]{2,1,0:T(8,128)(2,1)S(1)} copy-done((bf16[1,16,4096]{2,1,0:T(8,128)(2,1)S(1)}, bf16[1,16,4096]{2,1,0:T(8,128)(2,1)}, u32[]{:S(2)}) %copy-start.1) | copy-done | bytes 131096
  0.9 0.0 copy-start.2
  0.9 0.7 copy-done.2
  1.6 0.0 copy-start.3
  1.6 0.7 copy-done.3
  2.2 0.0 copy-start.4
  2.2 0.0 copy-start.5
  2.2 1.5 %shard_map.64 = bf16[64,40,128]{2,1,0:T(8,128)(2,1)} custom-call(s32[8]{0:T(128)S(1)} %copy-done.2, s32[64]{0:T(128)S(1)} %copy-done.3, bf16[1,16,4096]{2,1,0:T(8,128)(2,1)S(1)} %copy-done.1), custom_call_target="tpu_custom_call" | custom-call | tf_op jit(solution)/shard_map/pallas_call | solution.py:83
  3.7 14.6 %all-to-all-start = ((bf16[64,40,128]{2,1,0:T(8,128)(2,1)}), bf16[64,40,128]{2,1,0:T(8,128)(2,1)S(1)}, u32[]{:S(2)}, u32[]{:S(2)}) async-start(bf16[64,40,128]{2,1,0:T(8,128)(2,1)} %shard_map.64), calls=%async_computation | async-start | bytes 1310720 | tf_op jit(solution)/shard_map/all_to_all | solution.py:90
  18.3 20.1 %all-to-all-done.have_ref = bf16[64,40,128]{2,1,0:T(8,128)(2,1)S(1)} async-done(((bf16[64,40,128]{2,1,0:T(8,128)(2,1)}), bf16[64,40,128]{2,1,0:T(8,128)(2,1)S(1)}, u32[]{:S(2)}, u32[]{:S(2)}) %all-to-all-start) | async-done | bytes 655392 | tf_op jit(solution)/shard_map/all_to_all | solution.py:90
  38.5 0.1 reshape.8.asked_ref
  38.6 0.7 shard_map.65
  39.4 20.0 %all_to_all.15.needed_ref = bf16[16,256,128]{2,1,0:T(8,128)(2,1)S(1)} all-to-all(bf16[16,256,128]{2,1,0:T(8,128)(2,1)S(1)} %bitcast.2), channel_id=1, replica_groups={{0,12,24,36,192,204,216,228,384,396,408,420,576,588,600,612},{48,60,72,..., dimensions={0} | all-to-all | bytes 2097152 | tf_op jit(solution)/shard_map/all_to_all | solution.py:103
  59.4 0.0 copy-done.4
  59.4 0.0 copy-done.5
  59.4 0.0 copy-start
  59.4 2.2 %copy-done = bf16[8,64,4096]{2,1,0:T(8,128)(2,1)S(1)} copy-done((bf16[8,64,4096]{2,1,0:T(8,128)(2,1)S(1)}, bf16[8,64,4096]{2,1,0:T(8,128)(2,1)}, u32[]{:S(2)}) %copy-start) | copy-done | bytes 4194328
  61.6 1.8 %shard_map.66 = f32[12,8,128]{2,1,0:T(8,128)S(1)} custom-call(s32[8]{0:T(128)S(1)} %copy-done.4, s32[8]{0:T(128)S(1)} %copy-done.5, bf16[8,64,4096]{2,1,0:T(8,128)(2,1)S(1)} %copy-done, bf16[16,256,128]{2,1,0:T(8,128)(2,1)S(1)} %all_to_all.15.needed_ref), custom_call_target="tpu_custom_call" | custom-call | tf_op jit(solution)/shard_map/pallas_call | solution.py:105
  63.4 21.3 %all_to_all.16 = f32[12,8,128]{2,1,0:T(8,128)S(1)} all-to-all(f32[12,8,128]{2,1,0:T(8,128)S(1)} %shard_map.66), channel_id=1, replica_groups=mesh['wide'=64,'narrow'=12] {'narrow'}, dimensions={0} | all-to-all | bytes 98304 | tf_op jit(solution)/shard_map/all_to_all | solution.py:112
  84.7 0.1 fusion
  84.8 0.6 pad_maximum_fusion
  (4 shorter events, 0.1 us)
Async XLA Ops:
  0.0 0.9 %copy-start.1 = (bf16[1,16,4096]{2,1,0:T(8,128)(2,1)S(1)}, bf16[1,16,4096]{2,1,0:T(8,128)(2,1)}, u32[]{:S(2)}) copy-start(bf16[1,16,4096]{2,1,0:T(8,128)(2,1)} %amp_ref.1) | copy-start | bytes 393220
  0.9 0.7 copy-start.2
  1.6 0.7 copy-start.3
  2.2 57.2 %copy-start.4 = (s32[8]{0:T(128)S(1)}, s32[8]{0:T(128)}, u32[]{:S(2)}) copy-start(s32[8]{0:T(128)} %shape_ref.1) | copy-start | bytes 100
  2.2 57.2 %copy-start.5 = (s32[8]{0:T(128)S(1)}, s32[8]{0:T(128)}, u32[]{:S(2)}) copy-start(s32[8]{0:T(128)} %rows_ref.1) | copy-start | bytes 100
  3.7 34.8 %all-to-all-start = ((bf16[64,40,128]{2,1,0:T(8,128)(2,1)}), bf16[64,40,128]{2,1,0:T(8,128)(2,1)S(1)}, u32[]{:S(2)}, u32[]{:S(2)}) async-start(bf16[64,40,128]{2,1,0:T(8,128)(2,1)} %shard_map.64), calls=%async_computation | async-start | bytes 1310720 | tf_op jit(solution)/shard_map/all_to_all | solution.py:90
  59.4 2.2 %copy-start = (bf16[8,64,4096]{2,1,0:T(8,128)(2,1)S(1)}, bf16[8,64,4096]{2,1,0:T(8,128)(2,1)}, u32[]{:S(2)}) copy-start(bf16[8,64,4096]{2,1,0:T(8,128)(2,1)} %integrals_ref.1) | copy-start | bytes 12582916

commit v4 on v3

--- a/solution.py
+++ b/solution.py
@@ -9,6 +9,7 @@
 NEAR = YL * CORES
 GROUP = XS * NEAR
 LANES = 128
+ANY = pl.BlockSpec(memory_space=pl.ANY)
 VMEM = pl.BlockSpec(memory_space=pltpu.VMEM)
 SMEM = pl.BlockSpec(memory_space=pltpu.SMEM)
 
@@ -17,17 +18,32 @@
     return pltpu.CompilerParams(vmem_limit_bytes=mib * 1024 * 1024)
 
 
-def spread_kernel(cols_ref, owner_ref, amp_ref, out_ref):
+def stay(x):
+    return pltpu.with_memory_space_constraint(x, pltpu.HBM)
+
+
+def keep(x):
+    return pltpu.with_memory_space_constraint(x, pltpu.VMEM)
+
+
+def spread_kernel(cols_hbm, owner_hbm, amp_hbm, out_ref, cols_ref, owner_ref, amp_ref, sems):
+    pairs_of = ((cols_hbm, cols_ref), (owner_hbm, owner_ref), (amp_hbm, amp_ref))
+    copies = [pltpu.make_async_copy(src, dst, sems.at[i]) for i, (src, dst) in enumerate(pairs_of)]
+    for copy in copies:
+        copy.start()
     tasks = cols_ref.shape[0]
     _, pairs, depth = amp_ref.shape
     part = depth // GROUP
     payload = part // LANES * pairs
     rows = out_ref.shape[1] - payload
+    copies[0].wait()
+    copies[1].wait()
     lane = lax.broadcasted_iota(jnp.int32, (rows, LANES), 1)
     wanted = jnp.zeros((rows, LANES), jnp.float32)
     for s in range(tasks):
         wanted = jnp.where(lane == s, owner_ref[cols_ref[s]].astype(jnp.float32), wanted)
     wanted = wanted.astype(out_ref.dtype)
+    copies[2].wait()
     for j in range(GROUP):
         x, near = divmod(j, NEAR)
         for yh in range(YH):
@@ -40,12 +56,13 @@
 
 def select_kernel(asked_ref, have_ref, out_ref):
     payload = out_ref.shape[1]
-
-    def copy(i, carry):
-        out_ref[i] = have_ref[asked_ref[i], :payload, :]
-        return carry
-
-    lax.fori_loop(0, out_ref.shape[0], copy, 0, unroll=8)
+    tasks = out_ref.shape[0] // GROUP
+    yh = lax.rem(lax.div(lax.axis_index("wide"), NEAR), YH)
+    for j in range(GROUP):
+        x, near = divmod(j, NEAR)
+        w = (x * YH + yh) * NEAR + near
+        for s in range(tasks):
+            out_ref[j * tasks + s] = have_ref[asked_ref[w * tasks + s], :payload, :]
 
 
 def ladder_kernel(shape_ref, rows_ref, integrals_ref, needed_ref, out_ref):
@@ -83,22 +100,26 @@
     blocks = pl.pallas_call(
         spread_kernel,
         out_shape=jax.ShapeDtypeStruct((wide, payload + 8, LANES), kind),
-        in_specs=[SMEM, SMEM, VMEM],
+        in_specs=[ANY, ANY, ANY],
         out_specs=VMEM,
-        compiler_params=room(2),
-    )(task_cols, tile_owner, amplitudes)
+        scratch_shapes=[
+            pltpu.SMEM(task_cols.shape, jnp.int32),
+            pltpu.SMEM(tile_owner.shape, jnp.int32),
+            pltpu.VMEM(amplitudes.shape, kind),
+            pltpu.SemaphoreType.DMA((3,)),
+        ],
+        compiler_params=room(1),
+    )(stay(task_cols), stay(tile_owner), stay(amplitudes))
     have = lax.all_to_all(blocks, "wide", 0, 0, tiled=True)
 
-    yh = lax.div(lax.axis_index("wide"), NEAR) % YH
-    asked = have[:, payload, :tasks].reshape(XS, YH, NEAR, tasks)
-    asked = lax.dynamic_index_in_dim(asked, yh, 1, keepdims=False).reshape(GROUP * tasks)
+    asked = have[:, payload, :tasks].astype(jnp.int32).reshape(wide * tasks)
     chosen = pl.pallas_call(
         select_kernel,
         out_shape=jax.ShapeDtypeStruct((GROUP * tasks, payload, LANES), kind),
         in_specs=[SMEM, VMEM],
         out_specs=VMEM,
         compiler_params=room(3),
-    )(asked.astype(jnp.int32), have)
+    )(asked, have)
     chosen = chosen.reshape(GROUP, tasks * payload, LANES)
     needed = lax.all_to_all(chosen, "wide", 0, 0, axis_index_groups=groups, tiled=True)
 
@@ -107,7 +128,7 @@
         out_shape=jax.ShapeDtypeStruct((narrow, pairs // 2, 2 * width), jnp.float32),
         in_specs=[SMEM, SMEM, VMEM, VMEM],
         out_specs=VMEM,
-        compiler_params=room(6),
+        compiler_params=room(1),
     )(task_shape, task_rows, integrals, needed)
     rows = lax.all_to_all(rows, "narrow", 0, 0, tiled=True)
     total = jnp.sum(rows, axis=0)

time: 86 us -> 83.1 us (0.966)
  blocking collectives: 41.3 us -> 75.9 us
  waiting for transfers between devices: 20.1 us -> 0 us
  starting transfers between devices: 14.6 us -> 0 us
  local copies, waits for them, and re-layouts: 4.6 us -> 2.36 us
    all_to_all x0 -> x1, blocking collectives: none -> 33.9 us  [local(): have = lax.all_to_all(blocks, 'wide', 0, 0, tiled=True)]
    all_to_all x1 -> x0, waiting for transfers between devices: 20.1 us -> none  [local(): have = lax.all_to_all(blocks, 'wide', 0, 0, tiled=True)]
    all_to_all x1 -> x0, starting transfers between devices: 14.6 us -> none  [local(): have = lax.all_to_all(blocks, 'wide', 0, 0, tiled=True)]
    unnamed x13 -> x6, local copies, waits for them, and re-layouts: 4.41 us -> 2.2 us
  transfers between devices with their start and end apart: 1 -> 0, of which waited for: 1 -> 0; matrix products, arithmetic and copies ran while one was open for 0% -> 0% of each run, Pallas kernels for 0% -> 0%
where the time goes in v4:
time: 83.1 us; the launch traced here: 82.6 us
  blocking collectives  75.9 us (91%)
  Pallas kernels  3.56 us (4%)
  local copies, waits for them, and re-layouts  2.36 us (3%)
    all_to_all x1, blocking collectives, local(): have = lax.all_to_all(blocks, 'wide', 0, 0, tiled=True)  33.9 us
    all_to_all x1, blocking collectives, local(): rows = lax.all_to_all(rows, 'narrow', 0, 0, tiled=True)  21.9 us
    all_to_all x1, blocking collectives, local(): lax.all_to_all(chosen, 'wide', 0, 0, axis_index_groups=groups, tiled=True)  20 us
    unnamed x6, local copies, waits for them, and re-layouts  2.2 us
    pallas_call x1, Pallas kernels, local(): pl.pallas_call(ladder_kernel, out_shape=jax.ShapeDtypeStruct((narrow, pai...  1.8 us

profile of v4, /device:TPU:1, one launch (start us, length us, event | category | flops | bytes accessed | tf_op | source)
XLA Modules:
  0.0 82.6 jit_solution(17140454316470973863)
XLA Ops:
  0.0 0.0 copy-start.2
  0.0 0.0 copy-start.1
  0.0 1.0 %shard_map.64 = bf16[64,40,128]{2,1,0:T(8,128)(2,1)S(1)} custom-call(s32[8]{0:T(128)} %cols_hbm.1, s32[64]{0:T(128)} %owner_hbm.1, bf16[1,16,4096]{2,1,0:T(8,128)(2,1)} %amp_hbm.1), custom_call_target="tpu_custom_call" | custom-call | tf_op jit(solution)/shard_map/pallas_call | solution.py:100
  1.1 33.9 %all_to_all.15.have_ref = bf16[64,40,128]{2,1,0:T(8,128)(2,1)S(1)} all-to-all(bf16[64,40,128]{2,1,0:T(8,128)(2,1)S(1)} %shard_map.64), channel_id=1, replica_groups=mesh['wide'=64,'narrow'=12] {'wide'}, dimensions={0} | all-to-all | bytes 1310720 | tf_op jit(solution)/shard_map/all_to_all | solution.py:113
  35.0 0.1 fusion
  35.1 0.1 reshape.8.asked_ref
  35.2 0.7 shard_map.65
  35.9 20.0 %all_to_all.16.needed_ref = bf16[16,256,128]{2,1,0:T(8,128)(2,1)S(1)} all-to-all(bf16[16,256,128]{2,1,0:T(8,128)(2,1)S(1)} %bitcast.1), channel_id=1, replica_groups={{0,12,24,36,192,204,216,228,384,396,408,420,576,588,600,612},{48,60,72,..., dimensions={0} | all-to-all | bytes 2097152 | tf_op jit(solution)/shard_map/all_to_all | solution.py:124
  56.0 0.0 copy-done.2
  56.0 0.0 copy-done.1
  56.0 0.0 copy-start
  56.0 2.2 %copy-done = bf16[8,64,4096]{2,1,0:T(8,128)(2,1)S(1)} copy-done((bf16[8,64,4096]{2,1,0:T(8,128)(2,1)S(1)}, bf16[8,64,4096]{2,1,0:T(8,128)(2,1)}, u32[]{:S(2)}) %copy-start) | copy-done | bytes 4194328
  58.1 1.8 %shard_map.66 = f32[12,8,128]{2,1,0:T(8,128)S(1)} custom-call(s32[8]{0:T(128)S(1)} %copy-done.1, s32[8]{0:T(128)S(1)} %copy-done.2, bf16[8,64,4096]{2,1,0:T(8,128)(2,1)S(1)} %copy-done, bf16[16,256,128]{2,1,0:T(8,128)(2,1)S(1)} %all_to_all.16.needed_ref), custom_call_target="tpu_custom_call" | custom-call | tf_op jit(solution)/shard_map/pallas_call | solution.py:126
  59.9 21.9 %all_to_all.17 = f32[12,8,128]{2,1,0:T(8,128)S(1)} all-to-all(f32[12,8,128]{2,1,0:T(8,128)S(1)} %shard_map.66), channel_id=1, replica_groups=mesh['wide'=64,'narrow'=12] {'narrow'}, dimensions={0} | all-to-all | bytes 98304 | tf_op jit(solution)/shard_map/all_to_all | solution.py:133
  81.9 0.1 fusion.1
  81.9 0.6 pad_maximum_fusion
  (1 shorter events, 0.0 us)
Async XLA Ops:
  0.0 56.0 %copy-start.2 = (s32[8]{0:T(128)S(1)}, s32[8]{0:T(128)}, u32[]{:S(2)}) copy-start(s32[8]{0:T(128)} %rows_ref.1) | copy-start | bytes 100
  0.0 56.0 %copy-start.1 = (s32[8]{0:T(128)S(1)}, s32[8]{0:T(128)}, u32[]{:S(2)}) copy-start(s32[8]{0:T(128)} %shape_ref.1) | copy-start | bytes 100
  56.0 2.2 %copy-start = (bf16[8,64,4096]{2,1,0:T(8,128)(2,1)S(1)}, bf16[8,64,4096]{2,1,0:T(8,128)(2,1)}, u32[]{:S(2)}) copy-start(bf16[8,64,4096]{2,1,0:T(8,128)(2,1)} %integrals_ref.1) | copy-start | bytes 12582916

commit v5 on v4

--- a/solution.py
+++ b/solution.py
@@ -34,24 +34,24 @@
     tasks = cols_ref.shape[0]
     _, pairs, depth = amp_ref.shape
     part = depth // GROUP
-    payload = part // LANES * pairs
-    rows = out_ref.shape[1] - payload
+    payload = out_ref.shape[1] - 1
     copies[0].wait()
     copies[1].wait()
-    lane = lax.broadcasted_iota(jnp.int32, (rows, LANES), 1)
-    wanted = jnp.zeros((rows, LANES), jnp.float32)
+    lane = lax.broadcasted_iota(jnp.int32, (2, LANES), 1)
+    wanted = jnp.zeros((2, LANES), jnp.float32)
     for s in range(tasks):
         wanted = jnp.where(lane == s, owner_ref[cols_ref[s]].astype(jnp.float32), wanted)
     wanted = wanted.astype(out_ref.dtype)
     copies[2].wait()
     for j in range(GROUP):
         x, near = divmod(j, NEAR)
+        for h in range(part // LANES):
+            at = j * part + h * LANES
+            tile = amp_ref[0, :, at : at + LANES].reshape(pairs // 2, 2, LANES)
+            for yh in range(YH):
+                out_ref[(x * YH + yh) * NEAR + near, h * (pairs // 2) : (h + 1) * (pairs // 2)] = tile
         for yh in range(YH):
-            w = (x * YH + yh) * NEAR + near
-            for h in range(part // LANES):
-                at = j * part + h * LANES
-                out_ref[w, h * pairs : (h + 1) * pairs, :] = amp_ref[0, :, at : at + LANES]
-            out_ref[w, payload:, :] = wanted
+            out_ref[(x * YH + yh) * NEAR + near, payload] = wanted
 
 
 def select_kernel(asked_ref, have_ref, out_ref):
@@ -62,18 +62,19 @@
         x, near = divmod(j, NEAR)
         w = (x * YH + yh) * NEAR + near
         for s in range(tasks):
-            out_ref[j * tasks + s] = have_ref[asked_ref[w * tasks + s], :payload, :]
+            out_ref[j * tasks + s] = have_ref[asked_ref[w * tasks + s], :payload]
 
 
 def ladder_kernel(shape_ref, rows_ref, integrals_ref, needed_ref, out_ref):
     tasks, width, depth = integrals_ref.shape
-    members, per, _ = needed_ref.shape
+    members, per, _, _ = needed_ref.shape
     halves = depth // members // LANES
-    pairs = per // tasks // halves
+    duos = per // tasks // halves
+    pairs = 2 * duos
     out_ref[...] = jnp.zeros_like(out_ref)
     for t in range(tasks):
         chosen = [
-            needed_ref[j, (t * halves + h) * pairs : (t * halves + h + 1) * pairs, :]
+            needed_ref[j, (t * halves + h) * duos : (t * halves + h + 1) * duos].reshape(pairs, LANES)
             for j in range(members)
             for h in range(halves)
         ]
@@ -93,13 +94,13 @@
     pairs = amplitudes.shape[1]
     narrow = lax.axis_size("narrow")
     wide = lax.axis_size("wide")
-    payload = depth // GROUP // LANES * pairs
+    payload = depth // GROUP // LANES * pairs // 2
     kind = amplitudes.dtype
     groups = [[(x * YH + yh) * NEAR + near for x in range(XS) for near in range(NEAR)] for yh in range(YH)]
 
     blocks = pl.pallas_call(
         spread_kernel,
-        out_shape=jax.ShapeDtypeStruct((wide, payload + 8, LANES), kind),
+        out_shape=jax.ShapeDtypeStruct((wide, payload + 1, 2, LANES), kind),
         in_specs=[ANY, ANY, ANY],
         out_specs=VMEM,
         scratch_shapes=[
@@ -112,15 +113,15 @@
     )(stay(task_cols), stay(tile_owner), stay(amplitudes))
     have = lax.all_to_all(blocks, "wide", 0, 0, tiled=True)
 
-    asked = have[:, payload, :tasks].astype(jnp.int32).reshape(wide * tasks)
+    asked = have[:, payload, 0, :tasks].astype(jnp.int32).reshape(wide * tasks)
     chosen = pl.pallas_call(
         select_kernel,
-        out_shape=jax.ShapeDtypeStruct((GROUP * tasks, payload, LANES), kind),
+        out_shape=jax.ShapeDtypeStruct((GROUP * tasks, payload, 2, LANES), kind),
         in_specs=[SMEM, VMEM],
         out_specs=VMEM,
         compiler_params=room(3),
     )(asked, have)
-    chosen = chosen.reshape(GROUP, tasks * payload, LANES)
+    chosen = chosen.reshape(GROUP, tasks * payload, 2, LANES)
     needed = lax.all_to_all(chosen, "wide", 0, 0, axis_index_groups=groups, tiled=True)
 
     rows = pl.pallas_call(

time: 83.1 us -> 81.2 us (0.977)
  blocking collectives: 75.9 us -> 73.7 us
    all_to_all x1, blocking collectives: 33.9 us -> 31.9 us  [local(): have = lax.all_to_all(blocks, 'wide', 0, 0, tiled=True)]
where the time goes in v5:
time: 81.2 us; the launch traced here: 80.6 us
  blocking collectives  73.7 us (91%)
  Pallas kernels  3.8 us (5%)
  local copies, waits for them, and re-layouts  2.36 us (3%)
    all_to_all x1, blocking collectives, local(): have = lax.all_to_all(blocks, 'wide', 0, 0, tiled=True)  31.9 us
    all_to_all x1, blocking collectives, local(): rows = lax.all_to_all(rows, 'narrow', 0, 0, tiled=True)  21.9 us
    all_to_all x1, blocking collectives, local(): lax.all_to_all(chosen, 'wide', 0, 0, axis_index_groups=groups, tiled=True)  19.9 us
    unnamed x6, local copies, waits for them, and re-layouts  2.2 us
    pallas_call x1, Pallas kernels, local(): pl.pallas_call(ladder_kernel, out_shape=jax.ShapeDtypeStruct((narrow, pai...  1.8 us

profile of v5, /device:TPU:1, one launch (start us, length us, event | category | flops | bytes accessed | tf_op | source)
XLA Modules:
  0.0 80.6 jit_solution(10251492591349520613)
XLA Ops:
  0.0 0.0 copy-start.2
  0.0 0.0 copy-start.1
  0.0 1.3 %shard_map.64 = bf16[64,17,2,128]{3,2,1,0:T(2,128)(2,1)S(1)} custom-call(s32[8]{0:T(128)} %cols_hbm.1, s32[64]{0:T(128)} %owner_hbm.1, bf16[1,16,4096]{2,1,0:T(8,128)(2,1)} %amp_hbm.1), custom_call_target="tpu_custom_call" | custom-call | tf_op jit(solution)/shard_map/pallas_call | solution.py:101
  1.3 31.9 %all_to_all.15.have_ref = bf16[64,17,2,128]{3,2,1,0:T(2,128)(2,1)S(1)} all-to-all(bf16[64,17,2,128]{3,2,1,0:T(2,128)(2,1)S(1)} %shard_map.64), channel_id=1, replica_groups=mesh['wide'=64,'narrow'=12] {'wide'}, dimensions={0} | all-to-all | bytes 1114112 | tf_op jit(solution)/shard_map/all_to_all | solution.py:114
  33.2 0.1 fusion
  33.3 0.1 reshape.8.asked_ref
  33.4 0.7 shard_map.65
  34.1 19.9 %all_to_all.16.needed_ref = bf16[16,128,2,128]{3,2,1,0:T(2,128)(2,1)S(1)} all-to-all(bf16[16,128,2,128]{3,2,1,0:T(2,128)(2,1)S(1)} %bitcast.1), channel_id=1, replica_groups={{0,12,24,36,192,204,216,228,384,396,408,420,576,588,600,612},{48,60,72,..., dimensions={0} | all-to-all | bytes 2097152 | tf_op jit(solution)/shard_map/all_to_all | solution.py:125
  54.0 0.0 copy-done.2
  54.0 0.0 copy-done.1
  54.0 0.0 copy-start
  54.0 2.2 %copy-done = bf16[8,64,4096]{2,1,0:T(8,128)(2,1)S(1)} copy-done((bf16[8,64,4096]{2,1,0:T(8,128)(2,1)S(1)}, bf16[8,64,4096]{2,1,0:T(8,128)(2,1)}, u32[]{:S(2)}) %copy-start) | copy-done | bytes 4194328
  56.2 1.8 %shard_map.66 = f32[12,8,128]{2,1,0:T(8,128)S(1)} custom-call(s32[8]{0:T(128)S(1)} %copy-done.1, s32[8]{0:T(128)S(1)} %copy-done.2, bf16[8,64,4096]{2,1,0:T(8,128)(2,1)S(1)} %copy-done, bf16[16,128,2,128]{3,2,1,0:T(2,128)(2,1)S(1)} %all_to_all.16.needed_ref), custom_call_target="tpu_custom_call" | custom-call | tf_op jit(solution)/shard_map/pallas_call | solution.py:127
  58.0 21.9 %all_to_all.17 = f32[12,8,128]{2,1,0:T(8,128)S(1)} all-to-all(f32[12,8,128]{2,1,0:T(8,128)S(1)} %shard_map.66), channel_id=1, replica_groups=mesh['wide'=64,'narrow'=12] {'narrow'}, dimensions={0} | all-to-all | bytes 98304 | tf_op jit(solution)/shard_map/all_to_all | solution.py:134
  80.0 0.1 fusion.1
  80.0 0.6 pad_maximum_fusion
  (1 shorter events, 0.0 us)
Async XLA Ops:
  0.0 54.0 %copy-start.2 = (s32[8]{0:T(128)S(1)}, s32[8]{0:T(128)}, u32[]{:S(2)}) copy-start(s32[8]{0:T(128)} %rows_ref.1) | copy-start | bytes 100
  0.0 54.0 %copy-start.1 = (s32[8]{0:T(128)S(1)}, s32[8]{0:T(128)}, u32[]{:S(2)}) copy-start(s32[8]{0:T(128)} %shape_ref.1) | copy-start | bytes 100
  54.0 2.2 %copy-start = (bf16[8,64,4096]{2,1,0:T(8,128)(2,1)S(1)}, bf16[8,64,4096]{2,1,0:T(8,128)(2,1)}, u32[]{:S(2)}) copy-start(bf16[8,64,4096]{2,1,0:T(8,128)(2,1)} %integrals_ref.1) | copy-start | bytes 12582916

commit v6 on v5

--- a/solution.py
+++ b/solution.py
@@ -54,15 +54,20 @@
             out_ref[(x * YH + yh) * NEAR + near, payload] = wanted
 
 
-def select_kernel(asked_ref, have_ref, out_ref):
+def select_kernel(have_ref, out_ref, vector_ref, asked_ref, sem):
     payload = out_ref.shape[1]
     tasks = out_ref.shape[0] // GROUP
     yh = lax.rem(lax.div(lax.axis_index("wide"), NEAR), YH)
     for j in range(GROUP):
         x, near = divmod(j, NEAR)
-        w = (x * YH + yh) * NEAR + near
+        slots = have_ref[(x * YH + yh) * NEAR + near, payload]
+        vector_ref[2 * j : 2 * j + 2] = slots.astype(jnp.float32).astype(jnp.int32)
+    copy = pltpu.make_async_copy(vector_ref, asked_ref, sem)
+    copy.start()
+    copy.wait()
+    for j in range(GROUP):
         for s in range(tasks):
-            out_ref[j * tasks + s] = have_ref[asked_ref[w * tasks + s], :payload]
+            out_ref[j * tasks + s] = have_ref[asked_ref[2 * j, s], :payload]
 
 
 def ladder_kernel(shape_ref, rows_ref, integrals_ref, needed_ref, out_ref):
@@ -113,14 +118,18 @@
     )(stay(task_cols), stay(tile_owner), stay(amplitudes))
     have = lax.all_to_all(blocks, "wide", 0, 0, tiled=True)
 
-    asked = have[:, payload, 0, :tasks].astype(jnp.int32).reshape(wide * tasks)
     chosen = pl.pallas_call(
         select_kernel,
         out_shape=jax.ShapeDtypeStruct((GROUP * tasks, payload, 2, LANES), kind),
-        in_specs=[SMEM, VMEM],
+        in_specs=[VMEM],
         out_specs=VMEM,
-        compiler_params=room(3),
-    )(asked, have)
+        scratch_shapes=[
+            pltpu.VMEM((2 * GROUP, LANES), jnp.int32),
+            pltpu.SMEM((2 * GROUP, LANES), jnp.int32),
+            pltpu.SemaphoreType.DMA,
+        ],
+        compiler_params=room(1),
+    )(have)
     chosen = chosen.reshape(GROUP, tasks * payload, 2, LANES)
     needed = lax.all_to_all(chosen, "wide", 0, 0, axis_index_groups=groups, tiled=True)
 

time: 81.2 us -> 79.2 us (0.975)
  local copies, waits for them, and re-layouts: 2.36 us -> 0.09 us
    unnamed x6, local copies, waits for them, and re-layouts: 2.2 us -> 0.01 us
where the time goes in v6:
time: 79.2 us; the launch traced here: 78.7 us
  blocking collectives  73.7 us (93%)
  Pallas kernels  4.24 us (5%)
    all_to_all x1, blocking collectives, local(): have = lax.all_to_all(blocks, 'wide', 0, 0, tiled=True)  31.9 us
    all_to_all x1, blocking collectives, local(): rows = lax.all_to_all(rows, 'narrow', 0, 0, tiled=True)  21.9 us
    all_to_all x1, blocking collectives, local(): lax.all_to_all(chosen, 'wide', 0, 0, axis_index_groups=groups, tiled=True)  19.9 us
    pallas_call x1, Pallas kernels, local(): pl.pallas_call(ladder_kernel, out_shape=jax.ShapeDtypeStruct((narrow, pai...  1.91 us

profile of v6, /device:TPU:1, one launch (start us, length us, event | category | flops | bytes accessed | tf_op | source)
XLA Modules:
  0.0 78.7 jit_solution(1769662200643333218)
XLA Ops:
  0.0 0.0 copy-start.2
  0.0 0.0 copy-start.1
  0.0 0.0 copy-start
  0.0 1.4 %shard_map.64 = bf16[64,17,2,128]{3,2,1,0:T(2,128)(2,1)S(1)} custom-call(s32[8]{0:T(128)} %cols_hbm.1, s32[64]{0:T(128)} %owner_hbm.1, bf16[1,16,4096]{2,1,0:T(8,128)(2,1)} %amp_hbm.1), custom_call_target="tpu_custom_call" | custom-call | tf_op jit(solution)/shard_map/pallas_call | solution.py:106
  1.4 31.9 %all_to_all.15.have_ref = bf16[64,17,2,128]{3,2,1,0:T(2,128)(2,1)S(1)} all-to-all(bf16[64,17,2,128]{3,2,1,0:T(2,128)(2,1)S(1)} %shard_map.64), channel_id=1, replica_groups=mesh['wide'=64,'narrow'=12] {'wide'}, dimensions={0} | all-to-all | bytes 1114112 | tf_op jit(solution)/shard_map/all_to_all | solution.py:119
  33.3 0.9 %shard_map.65 = bf16[128,16,2,128]{3,2,1,0:T(2,128)(2,1)S(1)} custom-call(bf16[64,17,2,128]{3,2,1,0:T(2,128)(2,1)S(1)} %all_to_all.15.have_ref), custom_call_target="tpu_custom_call" | custom-call | tf_op jit(solution)/shard_map/pallas_call | solution.py:121
  34.3 19.9 %all_to_all.16.needed_ref = bf16[16,128,2,128]{3,2,1,0:T(2,128)(2,1)S(1)} all-to-all(bf16[16,128,2,128]{3,2,1,0:T(2,128)(2,1)S(1)} %bitcast.1), channel_id=1, replica_groups={{0,12,24,36,192,204,216,228,384,396,408,420,576,588,600,612},{48,60,72,..., dimensions={0} | all-to-all | bytes 2097152 | tf_op jit(solution)/shard_map/all_to_all | solution.py:134
  54.2 0.0 copy-done.2
  54.2 0.0 copy-done.1
  54.2 0.0 copy-done
  54.2 1.9 %shard_map.66 = f32[12,8,128]{2,1,0:T(8,128)S(1)} custom-call(s32[8]{0:T(128)S(1)} %copy-done.1, s32[8]{0:T(128)S(1)} %copy-done.2, bf16[8,64,4096]{2,1,0:T(8,128)(2,1)S(1)} %copy-done, bf16[16,128,2,128]{3,2,1,0:T(2,128)(2,1)S(1)} %all_to_all.16.needed_ref), custom_call_target="tpu_custom_call" | custom-call | tf_op jit(solution)/shard_map/pallas_call | solution.py:136
  56.1 21.9 %all_to_all.17 = f32[12,8,128]{2,1,0:T(8,128)S(1)} all-to-all(f32[12,8,128]{2,1,0:T(8,128)S(1)} %shard_map.66), channel_id=1, replica_groups=mesh['wide'=64,'narrow'=12] {'narrow'}, dimensions={0} | all-to-all | bytes 98304 | tf_op jit(solution)/shard_map/all_to_all | solution.py:143
  78.0 0.1 fusion
  78.1 0.6 pad_maximum_fusion
  (1 shorter events, 0.0 us)
Async XLA Ops:
  0.0 54.2 %copy-start.2 = (s32[8]{0:T(128)S(1)}, s32[8]{0:T(128)}, u32[]{:S(2)}) copy-start(s32[8]{0:T(128)} %rows_ref.1) | copy-start | bytes 100
  0.0 54.2 %copy-start.1 = (s32[8]{0:T(128)S(1)}, s32[8]{0:T(128)}, u32[]{:S(2)}) copy-start(s32[8]{0:T(128)} %shape_ref.1) | copy-start | bytes 100
  0.0 54.2 %copy-start = (bf16[8,64,4096]{2,1,0:T(8,128)(2,1)S(1)}, bf16[8,64,4096]{2,1,0:T(8,128)(2,1)}, u32[]{:S(2)}) copy-start(bf16[8,64,4096]{2,1,0:T(8,128)(2,1)} %integrals_ref.1) | copy-start | bytes 12582916

commit v7 on v6

--- a/solution.py
+++ b/solution.py
@@ -8,6 +8,7 @@
 XS, YH, YL, CORES = 4, 4, 2, 2
 NEAR = YL * CORES
 GROUP = XS * NEAR
+WIDE_FROM, GROUP_FROM, NARROW_FROM = 40, 8, 9
 LANES = 128
 ANY = pl.BlockSpec(memory_space=pl.ANY)
 VMEM = pl.BlockSpec(memory_space=pltpu.VMEM)
@@ -16,6 +17,10 @@
 
 def room(mib):
     return pltpu.CompilerParams(vmem_limit_bytes=mib * 1024 * 1024)
+
+
+def turned(devices, start):
+    return devices[start:] + devices[:start]
 
 
 def stay(x):
@@ -45,29 +50,33 @@
     copies[2].wait()
     for j in range(GROUP):
         x, near = divmod(j, NEAR)
+        places = [((x * YH + yh) * NEAR + near - WIDE_FROM) % out_ref.shape[0] for yh in range(YH)]
         for h in range(part // LANES):
             at = j * part + h * LANES
             tile = amp_ref[0, :, at : at + LANES].reshape(pairs // 2, 2, LANES)
-            for yh in range(YH):
-                out_ref[(x * YH + yh) * NEAR + near, h * (pairs // 2) : (h + 1) * (pairs // 2)] = tile
-        for yh in range(YH):
-            out_ref[(x * YH + yh) * NEAR + near, payload] = wanted
+            for place in places:
+                out_ref[place, h * (pairs // 2) : (h + 1) * (pairs // 2)] = tile
+        for place in places:
+            out_ref[place, payload] = wanted
 
 
 def select_kernel(have_ref, out_ref, vector_ref, asked_ref, sem):
     payload = out_ref.shape[1]
     tasks = out_ref.shape[0] // GROUP
+    wide = have_ref.shape[0]
+    back = wide - WIDE_FROM
     yh = lax.rem(lax.div(lax.axis_index("wide"), NEAR), YH)
     for j in range(GROUP):
         x, near = divmod(j, NEAR)
-        slots = have_ref[(x * YH + yh) * NEAR + near, payload]
+        slots = have_ref[lax.rem((x * YH + yh) * NEAR + near + back, wide), payload]
         vector_ref[2 * j : 2 * j + 2] = slots.astype(jnp.float32).astype(jnp.int32)
     copy = pltpu.make_async_copy(vector_ref, asked_ref, sem)
     copy.start()
     copy.wait()
     for j in range(GROUP):
         for s in range(tasks):
-            out_ref[j * tasks + s] = have_ref[asked_ref[2 * j, s], :payload]
+            place = (j - GROUP_FROM) % GROUP * tasks + s
+            out_ref[place] = have_ref[lax.rem(asked_ref[2 * j, s] + back, wide), :payload]
 
 
 def ladder_kernel(shape_ref, rows_ref, integrals_ref, needed_ref, out_ref):
@@ -76,10 +85,11 @@
     halves = depth // members // LANES
     duos = per // tasks // halves
     pairs = 2 * duos
+    narrow = out_ref.shape[0]
     out_ref[...] = jnp.zeros_like(out_ref)
     for t in range(tasks):
         chosen = [
-            needed_ref[j, (t * halves + h) * duos : (t * halves + h + 1) * duos].reshape(pairs, LANES)
+            needed_ref[(j - GROUP_FROM) % members, (t * halves + h) * duos : (t * halves + h + 1) * duos].reshape(pairs, LANES)
             for j in range(members)
             for h in range(halves)
         ]
@@ -91,7 +101,7 @@
         )
         live = lax.broadcasted_iota(jnp.int32, product.shape, 1) < shape_ref[t]
         product = jnp.where(live, product, 0.0)
-        out_ref[rows_ref[t]] += jnp.concatenate([product[: pairs // 2], product[pairs // 2 :]], axis=1)
+        out_ref[lax.rem(rows_ref[t] + narrow - NARROW_FROM, narrow)] += jnp.concatenate([product[: pairs // 2], product[pairs // 2 :]], axis=1)
 
 
 def local(integrals, task_shape, task_rows, task_cols, tile_owner, amplitudes):
@@ -102,6 +112,7 @@
     payload = depth // GROUP // LANES * pairs // 2
     kind = amplitudes.dtype
     groups = [[(x * YH + yh) * NEAR + near for x in range(XS) for near in range(NEAR)] for yh in range(YH)]
+    groups = [turned(group, GROUP_FROM) for group in groups]
 
     blocks = pl.pallas_call(
         spread_kernel,
@@ -116,7 +127,8 @@
         ],
         compiler_params=room(1),
     )(stay(task_cols), stay(tile_owner), stay(amplitudes))
-    have = lax.all_to_all(blocks, "wide", 0, 0, tiled=True)
+    everyone = [turned(list(range(wide)), WIDE_FROM)]
+    have = lax.all_to_all(blocks, "wide", 0, 0, axis_index_groups=everyone, tiled=True)
 
     chosen = pl.pallas_call(
         select_kernel,
@@ -140,7 +152,8 @@
         out_specs=VMEM,
         compiler_params=room(1),
     )(task_shape, task_rows, integrals, needed)
-    rows = lax.all_to_all(rows, "narrow", 0, 0, tiled=True)
+    column = [turned(list(range(narrow)), NARROW_FROM)]
+    rows = lax.all_to_all(rows, "narrow", 0, 0, axis_index_groups=column, tiled=True)
     total = jnp.sum(rows, axis=0)
     return jnp.concatenate([total[:, :width], total[:, width:]], axis=0)
 

time: 79.2 us -> 72.4 us (0.914)
  blocking collectives: 73.7 us -> 66.2 us
    all_to_all x2, blocking collectives: 53.8 us -> 47.1 us  [the longest x1 33.2 us: local(): lax.all_to_all(blocks, 'wide', 0, 0, axis_index_groups=everyone, tiled=True)]
where the time goes in v7:
time: 72.4 us; the launch traced here: 71.4 us
  blocking collectives  66.2 us (91%)
  Pallas kernels  4.5 us (6%)
    all_to_all x1, blocking collectives, local(): lax.all_to_all(blocks, 'wide', 0, 0, axis_index_groups=everyone, tiled=True)  33.2 us
    all_to_all x1, blocking collectives, local(): lax.all_to_all(chosen, 'wide', 0, 0, axis_index_groups=groups, tiled=True)  19.2 us
    all_to_all x1, blocking collectives, local(): lax.all_to_all(rows, 'narrow', 0, 0, axis_index_groups=column, tiled=True)  13.8 us
    pallas_call x1, Pallas kernels, local(): pl.pallas_call(ladder_kernel, out_shape=jax.ShapeDtypeStruct((narrow, pai...  1.92 us

profile of v7, /device:TPU:1, one launch (start us, length us, event | category | flops | bytes accessed | tf_op | source)
XLA Modules:
  0.0 71.4 jit_solution(13728949267659701334)
XLA Ops:
  0.0 0.0 copy-start.2
  0.0 0.0 copy-start.1
  0.0 0.0 copy-start
  0.0 1.4 %shard_map.64 = bf16[64,17,2,128]{3,2,1,0:T(2,128)(2,1)S(1)} custom-call(s32[8]{0:T(128)} %cols_hbm.1, s32[64]{0:T(128)} %owner_hbm.1, bf16[1,16,4096]{2,1,0:T(8,128)(2,1)} %amp_hbm.1), custom_call_target="tpu_custom_call" | custom-call | tf_op jit(solution)/shard_map/pallas_call | solution.py:117
  1.4 33.2 %all_to_all.15.have_ref = bf16[64,17,2,128]{3,2,1,0:T(2,128)(2,1)S(1)} all-to-all(bf16[64,17,2,128]{3,2,1,0:T(2,128)(2,1)S(1)} %shard_map.64), channel_id=1, replica_groups={{480,492,504,516,528,540,552,564,576,588,600,612,624,636,648,660,672,68..., dimensions={0} | all-to-all | bytes 1114112 | tf_op jit(solution)/shard_map/all_to_all | solution.py:131
  34.6 1.2 %shard_map.65 = bf16[128,16,2,128]{3,2,1,0:T(2,128)(2,1)S(1)} custom-call(bf16[64,17,2,128]{3,2,1,0:T(2,128)(2,1)S(1)} %all_to_all.15.have_ref), custom_call_target="tpu_custom_call" | custom-call | tf_op jit(solution)/shard_map/pallas_call | solution.py:133
  35.8 19.2 %all_to_all.16.needed_ref = bf16[16,128,2,128]{3,2,1,0:T(2,128)(2,1)S(1)} all-to-all(bf16[16,128,2,128]{3,2,1,0:T(2,128)(2,1)S(1)} %bitcast.1), channel_id=1, replica_groups={{384,396,408,420,576,588,600,612,0,12,24,36,192,204,216,228},{432,444,4..., dimensions={0} | all-to-all | bytes 2097152 | tf_op jit(solution)/shard_map/all_to_all | solution.py:146
  55.0 0.0 copy-done.2
  55.0 0.0 copy-done.1
  55.0 0.0 copy-done
  55.0 1.9 %shard_map.66 = f32[12,8,128]{2,1,0:T(8,128)S(1)} custom-call(s32[8]{0:T(128)S(1)} %copy-done.1, s32[8]{0:T(128)S(1)} %copy-done.2, bf16[8,64,4096]{2,1,0:T(8,128)(2,1)S(1)} %copy-done, bf16[16,128,2,128]{3,2,1,0:T(2,128)(2,1)S(1)} %all_to_all.16.needed_ref), custom_call_target="tpu_custom_call" | custom-call | tf_op jit(solution)/shard_map/pallas_call | solution.py:148
  56.9 13.8 %all_to_all.17 = f32[12,8,128]{2,1,0:T(8,128)S(1)} all-to-all(f32[12,8,128]{2,1,0:T(8,128)S(1)} %shard_map.66), channel_id=1, replica_groups={{9,10,11,0,1,2,3,4,5,6,7,8},{21,22,23,12,13,14,15,16,17,18,19,20},{33,3..., dimensions={0} | all-to-all | bytes 98304 | tf_op jit(solution)/shard_map/all_to_all | solution.py:156
  70.8 0.1 fusion
  70.8 0.6 pad_maximum_fusion
  (1 shorter events, 0.0 us)
Async XLA Ops:
  0.0 55.0 %copy-start.2 = (s32[8]{0:T(128)S(1)}, s32[8]{0:T(128)}, u32[]{:S(2)}) copy-start(s32[8]{0:T(128)} %rows_ref.1) | copy-start | bytes 100
  0.0 55.0 %copy-start.1 = (s32[8]{0:T(128)S(1)}, s32[8]{0:T(128)}, u32[]{:S(2)}) copy-start(s32[8]{0:T(128)} %shape_ref.1) | copy-start | bytes 100
  0.0 55.0 %copy-start = (bf16[8,64,4096]{2,1,0:T(8,128)(2,1)S(1)}, bf16[8,64,4096]{2,1,0:T(8,128)(2,1)}, u32[]{:S(2)}) copy-start(bf16[8,64,4096]{2,1,0:T(8,128)(2,1)} %integrals_ref.1) | copy-start | bytes 12582916

commit v8 on v7

--- a/solution.py
+++ b/solution.py
@@ -8,7 +8,8 @@
 XS, YH, YL, CORES = 4, 4, 2, 2
 NEAR = YL * CORES
 GROUP = XS * NEAR
-WIDE_FROM, GROUP_FROM, NARROW_FROM = 40, 8, 9
+WIDE_FROM, GROUP_FROM, NARROW_FROM = 41, 9, 9
+PIECES = 4
 LANES = 128
 ANY = pl.BlockSpec(memory_space=pl.ANY)
 VMEM = pl.BlockSpec(memory_space=pltpu.VMEM)
@@ -32,7 +33,10 @@
 
 
 def spread_kernel(cols_hbm, owner_hbm, amp_hbm, out_ref, cols_ref, owner_ref, amp_ref, sems):
-    pairs_of = ((cols_hbm, cols_ref), (owner_hbm, owner_ref), (amp_hbm, amp_ref))
+    width = amp_ref.shape[2] // PIECES
+    spans = [pl.ds(i * width, width) for i in range(PIECES)]
+    pairs_of = [(cols_hbm, cols_ref), (owner_hbm, owner_ref)]
+    pairs_of += [(amp_hbm.at[:, :, span], amp_ref.at[:, :, span]) for span in spans]
     copies = [pltpu.make_async_copy(src, dst, sems.at[i]) for i, (src, dst) in enumerate(pairs_of)]
     for copy in copies:
         copy.start()
@@ -47,8 +51,9 @@
     for s in range(tasks):
         wanted = jnp.where(lane == s, owner_ref[cols_ref[s]].astype(jnp.float32), wanted)
     wanted = wanted.astype(out_ref.dtype)
-    copies[2].wait()
     for j in range(GROUP):
+        if j % (GROUP // PIECES) == 0:
+            copies[2 + j * PIECES // GROUP].wait()
         x, near = divmod(j, NEAR)
         places = [((x * YH + yh) * NEAR + near - WIDE_FROM) % out_ref.shape[0] for yh in range(YH)]
         for h in range(part // LANES):
@@ -69,14 +74,15 @@
     for j in range(GROUP):
         x, near = divmod(j, NEAR)
         slots = have_ref[lax.rem((x * YH + yh) * NEAR + near + back, wide), payload]
-        vector_ref[2 * j : 2 * j + 2] = slots.astype(jnp.float32).astype(jnp.int32)
+        slots = slots.astype(jnp.float32).astype(jnp.int32) + back
+        vector_ref[2 * j : 2 * j + 2] = jnp.where(slots < wide, slots, slots - wide)
     copy = pltpu.make_async_copy(vector_ref, asked_ref, sem)
     copy.start()
     copy.wait()
     for j in range(GROUP):
         for s in range(tasks):
             place = (j - GROUP_FROM) % GROUP * tasks + s
-            out_ref[place] = have_ref[lax.rem(asked_ref[2 * j, s] + back, wide), :payload]
+            out_ref[place] = have_ref[asked_ref[2 * j, s], :payload]
 
 
 def ladder_kernel(shape_ref, rows_ref, integrals_ref, needed_ref, out_ref):
@@ -123,7 +129,7 @@
             pltpu.SMEM(task_cols.shape, jnp.int32),
             pltpu.SMEM(tile_owner.shape, jnp.int32),
             pltpu.VMEM(amplitudes.shape, kind),
-            pltpu.SemaphoreType.DMA((3,)),
+            pltpu.SemaphoreType.DMA((2 + PIECES,)),
         ],
         compiler_params=room(1),
     )(stay(task_cols), stay(tile_owner), stay(amplitudes))

time: 72.4 us -> 71.5 us (0.988)
  no operation moved by 1% of the time
where the time goes in v8:
time: 71.5 us; the launch traced here: 70.5 us
  blocking collectives  65.6 us (92%)
  Pallas kernels  4.15 us (6%)
    all_to_all x1, blocking collectives, local(): lax.all_to_all(blocks, 'wide', 0, 0, axis_index_groups=everyone, tiled=True)  33.1 us
    all_to_all x1, blocking collectives, local(): lax.all_to_all(chosen, 'wide', 0, 0, axis_index_groups=groups, tiled=True)  18.8 us
    all_to_all x1, blocking collectives, local(): lax.all_to_all(rows, 'narrow', 0, 0, axis_index_groups=column, tiled=True)  13.7 us
    pallas_call x1, Pallas kernels, local(): pl.pallas_call(ladder_kernel, out_shape=jax.ShapeDtypeStruct((narrow, pai...  1.92 us

profile of v8, /device:TPU:1, one launch (start us, length us, event | category | flops | bytes accessed | tf_op | source)
XLA Modules:
  0.0 70.5 jit_solution(7964222158566340540)
XLA Ops:
  0.0 0.0 copy-start.2
  0.0 0.0 copy-start.1
  0.0 0.0 copy-start
  0.0 1.3 %shard_map.64 = bf16[64,17,2,128]{3,2,1,0:T(2,128)(2,1)S(1)} custom-call(s32[8]{0:T(128)} %cols_hbm.1, s32[64]{0:T(128)} %owner_hbm.1, bf16[1,16,4096]{2,1,0:T(8,128)(2,1)} %amp_hbm.1), custom_call_target="tpu_custom_call" | custom-call | tf_op jit(solution)/shard_map/pallas_call | solution.py:123
  1.3 33.1 %all_to_all.15.have_ref = bf16[64,17,2,128]{3,2,1,0:T(2,128)(2,1)S(1)} all-to-all(bf16[64,17,2,128]{3,2,1,0:T(2,128)(2,1)S(1)} %shard_map.64), channel_id=1, replica_groups={{492,504,516,528,540,552,564,576,588,600,612,624,636,648,660,672,684,69..., dimensions={0} | all-to-all | bytes 1114112 | tf_op jit(solution)/shard_map/all_to_all | solution.py:137
  34.4 0.9 %shard_map.65 = bf16[128,16,2,128]{3,2,1,0:T(2,128)(2,1)S(1)} custom-call(bf16[64,17,2,128]{3,2,1,0:T(2,128)(2,1)S(1)} %all_to_all.15.have_ref), custom_call_target="tpu_custom_call" | custom-call | tf_op jit(solution)/shard_map/pallas_call | solution.py:139
  35.4 18.8 %all_to_all.16.needed_ref = bf16[16,128,2,128]{3,2,1,0:T(2,128)(2,1)S(1)} all-to-all(bf16[16,128,2,128]{3,2,1,0:T(2,128)(2,1)S(1)} %bitcast.1), channel_id=1, replica_groups={{396,408,420,576,588,600,612,0,12,24,36,192,204,216,228,384},{444,456,4..., dimensions={0} | all-to-all | bytes 2097152 | tf_op jit(solution)/shard_map/all_to_all | solution.py:152
  54.2 0.0 copy-done.2
  54.2 0.0 copy-done.1
  54.2 0.0 copy-done
  54.2 1.9 %shard_map.66 = f32[12,8,128]{2,1,0:T(8,128)S(1)} custom-call(s32[8]{0:T(128)S(1)} %copy-done.1, s32[8]{0:T(128)S(1)} %copy-done.2, bf16[8,64,4096]{2,1,0:T(8,128)(2,1)S(1)} %copy-done, bf16[16,128,2,128]{3,2,1,0:T(2,128)(2,1)S(1)} %all_to_all.16.needed_ref), custom_call_target="tpu_custom_call" | custom-call | tf_op jit(solution)/shard_map/pallas_call | solution.py:154
  56.1 13.7 %all_to_all.17 = f32[12,8,128]{2,1,0:T(8,128)S(1)} all-to-all(f32[12,8,128]{2,1,0:T(8,128)S(1)} %shard_map.66), channel_id=1, replica_groups={{9,10,11,0,1,2,3,4,5,6,7,8},{21,22,23,12,13,14,15,16,17,18,19,20},{33,3..., dimensions={0} | all-to-all | bytes 98304 | tf_op jit(solution)/shard_map/all_to_all | solution.py:162
  69.8 0.1 fusion
  69.9 0.6 pad_maximum_fusion
  (1 shorter events, 0.0 us)
Async XLA Ops:
  0.0 54.2 %copy-start.2 = (s32[8]{0:T(128)S(1)}, s32[8]{0:T(128)}, u32[]{:S(2)}) copy-start(s32[8]{0:T(128)} %rows_ref.1) | copy-start | bytes 100
  0.0 54.2 %copy-start.1 = (s32[8]{0:T(128)S(1)}, s32[8]{0:T(128)}, u32[]{:S(2)}) copy-start(s32[8]{0:T(128)} %shape_ref.1) | copy-start | bytes 100
  0.0 54.2 %copy-start = (bf16[8,64,4096]{2,1,0:T(8,128)(2,1)S(1)}, bf16[8,64,4096]{2,1,0:T(8,128)(2,1)}, u32[]{:S(2)}) copy-start(bf16[8,64,4096]{2,1,0:T(8,128)(2,1)} %integrals_ref.1) | copy-start | bytes 12582916

commit v9 on v8

--- a/solution.py
+++ b/solution.py
@@ -49,7 +49,7 @@
     lane = lax.broadcasted_iota(jnp.int32, (2, LANES), 1)
     wanted = jnp.zeros((2, LANES), jnp.float32)
     for s in range(tasks):
-        wanted = jnp.where(lane == s, owner_ref[cols_ref[s]].astype(jnp.float32), wanted)
+        wanted = jnp.where(lane % tasks == s, owner_ref[cols_ref[s]].astype(jnp.float32), wanted)
     wanted = wanted.astype(out_ref.dtype)
     for j in range(GROUP):
         if j % (GROUP // PIECES) == 0:
@@ -71,18 +71,21 @@
     wide = have_ref.shape[0]
     back = wide - WIDE_FROM
     yh = lax.rem(lax.div(lax.axis_index("wide"), NEAR), YH)
+    member = lax.broadcasted_iota(jnp.int32, (2, LANES), 1) // tasks
+    asked = jnp.zeros((2, LANES), jnp.float32)
     for j in range(GROUP):
         x, near = divmod(j, NEAR)
         slots = have_ref[lax.rem((x * YH + yh) * NEAR + near + back, wide), payload]
-        slots = slots.astype(jnp.float32).astype(jnp.int32) + back
-        vector_ref[2 * j : 2 * j + 2] = jnp.where(slots < wide, slots, slots - wide)
+        asked = jnp.where(member == j, slots.astype(jnp.float32), asked)
+    asked = asked.astype(jnp.int32) + back
+    vector_ref[...] = jnp.where(asked < wide, asked, asked - wide)
     copy = pltpu.make_async_copy(vector_ref, asked_ref, sem)
     copy.start()
     copy.wait()
     for j in range(GROUP):
         for s in range(tasks):
             place = (j - GROUP_FROM) % GROUP * tasks + s
-            out_ref[place] = have_ref[asked_ref[2 * j, s], :payload]
+            out_ref[place] = have_ref[asked_ref[0, j * tasks + s], :payload]
 
 
 def ladder_kernel(shape_ref, rows_ref, integrals_ref, needed_ref, out_ref):
@@ -142,8 +145,8 @@
         in_specs=[VMEM],
         out_specs=VMEM,
         scratch_shapes=[
-            pltpu.VMEM((2 * GROUP, LANES), jnp.int32),
-            pltpu.SMEM((2 * GROUP, LANES), jnp.int32),
+            pltpu.VMEM((2, GROUP * tasks), jnp.int32),
+            pltpu.SMEM((2, GROUP * tasks), jnp.int32),
             pltpu.SemaphoreType.DMA,
         ],
         compiler_params=room(1),

time: 71.5 us -> 71.2 us (level)
  no operation moved by 1% of the time
where the time goes in v9:
time: 71.2 us; the launch traced here: 70.2 us
  blocking collectives  65.6 us (92%)
  Pallas kernels  3.91 us (5%)
    all_to_all x1, blocking collectives, local(): lax.all_to_all(blocks, 'wide', 0, 0, axis_index_groups=everyone, tiled=True)  33.1 us
    all_to_all x1, blocking collectives, local(): lax.all_to_all(chosen, 'wide', 0, 0, axis_index_groups=groups, tiled=True)  18.8 us
    all_to_all x1, blocking collectives, local(): lax.all_to_all(rows, 'narrow', 0, 0, axis_index_groups=column, tiled=True)  13.6 us
    pallas_call x1, Pallas kernels, local(): pl.pallas_call(ladder_kernel, out_shape=jax.ShapeDtypeStruct((narrow, pai...  1.92 us

profile of v9, /device:TPU:1, one launch (start us, length us, event | category | flops | bytes accessed | tf_op | source)
XLA Modules:
  0.0 70.2 jit_solution(2495388800050032531)
XLA Ops:
  0.0 0.0 copy-start.2
  0.0 0.0 copy-start.1
  0.0 0.0 copy-start
  0.0 1.3 %shard_map.64 = bf16[64,17,2,128]{3,2,1,0:T(2,128)(2,1)S(1)} custom-call(s32[8]{0:T(128)} %cols_hbm.1, s32[64]{0:T(128)} %owner_hbm.1, bf16[1,16,4096]{2,1,0:T(8,128)(2,1)} %amp_hbm.1), custom_call_target="tpu_custom_call" | custom-call | tf_op jit(solution)/shard_map/pallas_call | solution.py:126
  1.3 33.1 %all_to_all.15.have_ref = bf16[64,17,2,128]{3,2,1,0:T(2,128)(2,1)S(1)} all-to-all(bf16[64,17,2,128]{3,2,1,0:T(2,128)(2,1)S(1)} %shard_map.64), channel_id=1, replica_groups={{492,504,516,528,540,552,564,576,588,600,612,624,636,648,660,672,684,69..., dimensions={0} | all-to-all | bytes 1114112 | tf_op jit(solution)/shard_map/all_to_all | solution.py:140
  34.4 0.7 shard_map.65
  35.1 18.8 %all_to_all.16.needed_ref = bf16[16,128,2,128]{3,2,1,0:T(2,128)(2,1)S(1)} all-to-all(bf16[16,128,2,128]{3,2,1,0:T(2,128)(2,1)S(1)} %bitcast.1), channel_id=1, replica_groups={{396,408,420,576,588,600,612,0,12,24,36,192,204,216,228,384},{444,456,4..., dimensions={0} | all-to-all | bytes 2097152 | tf_op jit(solution)/shard_map/all_to_all | solution.py:155
  54.0 0.0 copy-done.2
  54.0 0.0 copy-done.1
  54.0 0.0 copy-done
  54.0 1.9 %shard_map.66 = f32[12,8,128]{2,1,0:T(8,128)S(1)} custom-call(s32[8]{0:T(128)S(1)} %copy-done.1, s32[8]{0:T(128)S(1)} %copy-done.2, bf16[8,64,4096]{2,1,0:T(8,128)(2,1)S(1)} %copy-done, bf16[16,128,2,128]{3,2,1,0:T(2,128)(2,1)S(1)} %all_to_all.16.needed_ref), custom_call_target="tpu_custom_call" | custom-call | tf_op jit(solution)/shard_map/pallas_call | solution.py:157
  55.9 13.6 %all_to_all.17 = f32[12,8,128]{2,1,0:T(8,128)S(1)} all-to-all(f32[12,8,128]{2,1,0:T(8,128)S(1)} %shard_map.66), channel_id=1, replica_groups={{9,10,11,0,1,2,3,4,5,6,7,8},{21,22,23,12,13,14,15,16,17,18,19,20},{33,3..., dimensions={0} | all-to-all | bytes 98304 | tf_op jit(solution)/shard_map/all_to_all | solution.py:165
  69.5 0.1 fusion
  69.6 0.6 pad_maximum_fusion
  (1 shorter events, 0.0 us)
Async XLA Ops:
  0.0 54.0 %copy-start.2 = (s32[8]{0:T(128)S(1)}, s32[8]{0:T(128)}, u32[]{:S(2)}) copy-start(s32[8]{0:T(128)} %rows_ref.1) | copy-start | bytes 100
  0.0 54.0 %copy-start.1 = (s32[8]{0:T(128)S(1)}, s32[8]{0:T(128)}, u32[]{:S(2)}) copy-start(s32[8]{0:T(128)} %shape_ref.1) | copy-start | bytes 100
  0.0 54.0 %copy-start = (bf16[8,64,4096]{2,1,0:T(8,128)(2,1)S(1)}, bf16[8,64,4096]{2,1,0:T(8,128)(2,1)}, u32[]{:S(2)}) copy-start(bf16[8,64,4096]{2,1,0:T(8,128)(2,1)} %integrals_ref.1) | copy-start | bytes 12582916
